TPU v7x, 256 devices: a whole 4x4x8 slice. The times are simulated.
256 devices in a mesh: seq: 32 (over z_lo, y, x), head: 8 (over z_hi, core).
Axes of the slice: x: 4, y: 4, z: 8 (z_hi: 4, z_lo: 2; z = z_hi * 2 + z_lo), core: 2. Of those that a mesh axis runs over, the one named last changes fastest.
Arguments:
- prompt_q: bfloat16 [2048, 8192], P(('seq', 'head')), may hold values from -100 to 100
- prompt_k: bfloat16 [2048, 1024], P(('seq', 'head')), may hold values from -4 to 4
- prompt_v: bfloat16 [2048, 1024], P(('seq', 'head')), may hold values from -6 to 6
- prompt_dout: bfloat16 [2048, 8192], P(('seq', 'head')), may hold values from -6 to 6
- cand_q: bfloat16 [8192, 8192], P(('seq', 'head')), may hold values from -100 to 100
- cand_k: bfloat16 [8192, 1024], P(('seq', 'head')), may hold values from -6 to 6
- cand_v: bfloat16 [8192, 1024], P(('seq', 'head')), may hold values from -6 to 6
- cand_dout: bfloat16 [8192, 8192], P(('seq', 'head')), may hold values from -6 to 6
- cand_len: int32 [16], replicated, may hold values from 128 to 512, as said below
- placement: int32 [16], replicated, may hold values from 0 to 15, each once
Outputs:
- prompt_out: bfloat16 [2048, 8192], P(('seq', 'head'))
- prompt_dq: bfloat16 [2048, 8192], P(('seq', 'head'))
- prompt_dk: bfloat16 [2048, 1024], P(('seq', 'head'))
- prompt_dv: bfloat16 [2048, 1024], P(('seq', 'head'))
- cand_out: bfloat16 [8192, 8192], P(('seq', 'head'))
- cand_dq: bfloat16 [8192, 8192], P(('seq', 'head'))
- cand_dk: bfloat16 [8192, 1024], P(('seq', 'head'))
- cand_dv: bfloat16 [8192, 1024], P(('seq', 'head'))
Inputs may be any that keep to these rules, and one draw needn't show every extreme that they name: `cand_len`: some candidate has 512 tokens and some has 128.
All inputs are finite; a program needn't handle non-finite values.
Results may differ from a plain program's by a relative error of at most 0.012.
The roundings to bfloat16 on the way count: a program that leaves them out, or rounds other values in their place, can miss the bound.
Values may be sent and summed in bfloat16 or wider, within the bound.
A program may use at most 64 MiB of HBM per device.

v0:
```python
import math

import jax
import jax.numpy as jnp
from jax import lax
from jax.sharding import PartitionSpec as P

HD = 128


def shifted(value, axis, steps):
    count = lax.axis_size(axis)
    leading, last = (max(0, -steps), min(count, count - steps))
    return lax.ppermute(value, axis, [(source, source + steps) for source in range(leading, last)])


def head_pass(queries, key_rows, value_rows, out_grads, allowed, is_valid):
    scaling = 1.0 / math.sqrt(queries.shape[-1])
    scores = jnp.dot(queries, key_rows.T, preferred_element_type=jnp.float32) * scaling
    scores = jnp.where(allowed, scores, -1e30)
    row_peak = jnp.max(scores, axis=1, keepdims=True)
    row_total = jnp.sum(jnp.exp(scores - row_peak), axis=1, keepdims=True)
    log_total = row_peak + jnp.log(row_total)
    weights = jnp.exp(scores - log_total)
    weight_half = weights.astype(jnp.bfloat16)
    product = jnp.dot(weight_half, value_rows, preferred_element_type=jnp.float32)
    output = jnp.where(is_valid[:, None], product, 0.0)
    row_delta = jnp.sum(out_grads.astype(jnp.float32) * output, axis=1, keepdims=True)
    grad_weights = jnp.dot(out_grads, value_rows.T, preferred_element_type=jnp.float32)
    grad_scores = (weights * (grad_weights - row_delta)).astype(jnp.bfloat16)
    query_grad = (
        scaling * jnp.dot(grad_scores, key_rows, preferred_element_type=jnp.float32)
    ).astype(jnp.bfloat16)
    key_grad = scaling * jnp.dot(grad_scores.T, queries, preferred_element_type=jnp.float32)
    value_grad = jnp.dot(weight_half.T, out_grads, preferred_element_type=jnp.float32)
    return (output.astype(jnp.bfloat16), query_grad, key_grad, value_grad)


def local(
    prompt_q,
    prompt_k,
    prompt_v,
    prompt_dout,
    cand_q,
    cand_k,
    cand_v,
    cand_dout,
    cand_len,
    placement,
):
    (
        prompt_query,
        prompt_key,
        prompt_value,
        prompt_grad,
        cand_query,
        cand_key,
        cand_value,
        cand_grad,
    ) = (
        lax.all_to_all(prompt_q, "head", split_axis=1, concat_axis=0, tiled=True),
        lax.all_to_all(prompt_k, "head", split_axis=1, concat_axis=0, tiled=True),
        lax.all_to_all(prompt_v, "head", split_axis=1, concat_axis=0, tiled=True),
        lax.all_to_all(prompt_dout, "head", split_axis=1, concat_axis=0, tiled=True),
        lax.all_to_all(cand_q, "head", split_axis=1, concat_axis=0, tiled=True),
        lax.all_to_all(cand_k, "head", split_axis=1, concat_axis=0, tiled=True),
        lax.all_to_all(cand_v, "head", split_axis=1, concat_axis=0, tiled=True),
        lax.all_to_all(cand_dout, "head", split_axis=1, concat_axis=0, tiled=True),
    )
    all_keys, all_values = (
        lax.all_gather(prompt_key, "seq", axis=0, tiled=True),
        lax.all_gather(prompt_value, "seq", axis=0, tiled=True),
    )
    before_keys, before_values = shifted((cand_key, cand_value), "seq", 1)
    device = lax.axis_index("seq")
    second_half = device % 2
    slot_index = device // 2
    prompt_dev = prompt_query.shape[0]
    cand_dev = cand_query.shape[0]
    prompt_all = all_keys.shape[0]
    slot_length = jnp.sum(jnp.where(placement == slot_index, cand_len, 0))
    local_rows = jnp.arange(cand_dev, dtype=jnp.int32)
    position = second_half * cand_dev + local_rows
    is_valid = jnp.concatenate([jnp.ones((prompt_dev,), bool), position < slot_length])
    prompt_global = device * prompt_dev + jnp.arange(prompt_dev, dtype=jnp.int32)
    key_index = jnp.arange(prompt_all, dtype=jnp.int32)
    upper_rows = jnp.concatenate(
        [key_index[None, :] <= prompt_global[:, None], jnp.zeros((prompt_dev, 2 * cand_dev), bool)],
        axis=1,
    )
    lower_rows = jnp.concatenate(
        [
            jnp.ones((cand_dev, prompt_all), bool),
            jnp.broadcast_to(second_half == 1, (cand_dev, cand_dev)),
            local_rows[None, :] <= local_rows[:, None],
        ],
        axis=1,
    )
    allowed = jnp.concatenate([upper_rows, lower_rows], axis=0)
    key_rows = jnp.concatenate([all_keys, before_keys, cand_key], axis=0)
    value_rows = jnp.concatenate([all_values, before_values, cand_value], axis=0)
    queries = jnp.concatenate([prompt_query, cand_query], axis=0)
    joined_grads = jnp.concatenate([prompt_grad, cand_grad], axis=0)
    live_grads = jnp.where(is_valid[:, None], joined_grads, jnp.zeros_like(joined_grads))
    query_heads = queries.shape[1] // HD
    total_rows = queries.shape[0]

    def per_head(carry, head_index):
        acc_keys, acc_values = carry
        column = head_index * HD
        one_query = lax.dynamic_slice_in_dim(queries, column, HD, 1)
        one_grad = lax.dynamic_slice_in_dim(live_grads, column, HD, 1)
        output, query_grad, key_grad, value_grad = head_pass(
            one_query, key_rows, value_rows, one_grad, allowed, is_valid
        )
        acc_keys = acc_keys + key_grad
        acc_values = acc_values + value_grad
        return ((acc_keys, acc_values), (output, query_grad))

    start = (jnp.zeros(key_rows.shape, jnp.float32), jnp.zeros(value_rows.shape, jnp.float32))
    (acc_keys, acc_values), (outputs, query_grads) = lax.scan(
        per_head, start, jnp.arange(query_heads, dtype=jnp.int32)
    )
    outputs = jnp.transpose(outputs, (1, 0, 2)).reshape(total_rows, query_heads * HD)
    query_grads = jnp.transpose(query_grads, (1, 0, 2)).reshape(total_rows, query_heads * HD)
    total_keys, total_values = lax.psum((acc_keys[:prompt_all], acc_values[:prompt_all]), "seq")
    prompt_key_grad = lax.dynamic_slice_in_dim(total_keys, device * prompt_dev, prompt_dev, 0)
    prompt_value_grad = lax.dynamic_slice_in_dim(total_values, device * prompt_dev, prompt_dev, 0)
    later_keys, later_values = shifted(
        (
            acc_keys[prompt_all : prompt_all + cand_dev],
            acc_values[prompt_all : prompt_all + cand_dev],
        ),
        "seq",
        -1,
    )
    cand_key_grad = (acc_keys[prompt_all + cand_dev :] + later_keys).astype(jnp.bfloat16)
    cand_value_grad = (acc_values[prompt_all + cand_dev :] + later_values).astype(jnp.bfloat16)
    return (
        lax.all_to_all(outputs[:prompt_dev], "head", split_axis=0, concat_axis=1, tiled=True),
        lax.all_to_all(query_grads[:prompt_dev], "head", split_axis=0, concat_axis=1, tiled=True),
        lax.all_to_all(
            prompt_key_grad.astype(jnp.bfloat16), "head", split_axis=0, concat_axis=1, tiled=True
        ),
        lax.all_to_all(
            prompt_value_grad.astype(jnp.bfloat16), "head", split_axis=0, concat_axis=1, tiled=True
        ),
        lax.all_to_all(outputs[prompt_dev:], "head", split_axis=0, concat_axis=1, tiled=True),
        lax.all_to_all(query_grads[prompt_dev:], "head", split_axis=0, concat_axis=1, tiled=True),
        lax.all_to_all(cand_key_grad, "head", split_axis=0, concat_axis=1, tiled=True),
        lax.all_to_all(cand_value_grad, "head", split_axis=0, concat_axis=1, tiled=True),
    )


def solution(mesh):
    placed = (
        P(("seq", "head"), None),
        P(("seq", "head"), None),
        P(("seq", "head"), None),
        P(("seq", "head"), None),
        P(("seq", "head"), None),
        P(("seq", "head"), None),
        P(("seq", "head"), None),
        P(("seq", "head"), None),
        P(),
        P(),
    )
    return jax.shard_map(
        local,
        mesh=mesh,
        in_specs=placed,
        out_specs=(
            P(("seq", "head"), None),
            P(("seq", "head"), None),
            P(("seq", "head"), None),
            P(("seq", "head"), None),
            P(("seq", "head"), None),
            P(("seq", "head"), None),
            P(("seq", "head"), None),
            P(("seq", "head"), None),
        ),
        check_vma=False,
    )
```

profile of v0, /device:TPU:1, one launch (start us, length us, event | category | flops | bytes accessed | tf_op | source)
XLA Modules:
  0.0 692.0 jit_solution(4022714636795084548)
XLA Ops:
  0.7 17.2 %all_to_all.304 = bf16[8,8,128]{2,0,1:T(8,128)(2,1)S(1)} all-to-all(bf16[8,8,128]{2,0,1:T(8,128)(2,1)} %bitcast.138), channel_id=1, replica_groups=mesh['seq'=32,'head'=8] {'head'}, dimensions={1} | all-to-all | bytes 32768 | tf_op jit(solution)/shard_map/all_to_all | solution.py:62
  17.9 4.0 all-to-all-start.6
  22.5 6.5 all-to-all-done.6
  29.5 4.0 all-to-all-start.3
  34.4 6.7 all-to-all-done.3
  41.1 11.1 %all_to_all.305 = bf16[32,8,128]{2,0,1:T(8,128)(2,1)} all-to-all(bf16[32,8,128]{2,0,1:T(8,128)(2,1)S(1)} %copy_bitcast_fusion.4), channel_id=1, replica_groups=mesh['seq'=32,'head'=8] {'head'}, dimensions={1} | all-to-all | bytes 131072 | tf_op jit(solution)/shard_map/all_to_all | solution.py:67
  52.2 4.3 all-to-all-start
  57.9 6.7 all-to-all-done
  64.6 4.9 all-to-all-start.4
  70.7 1.9 copy.83
  75.8 1.8 all-to-all-done.4
  78.2 5.5 all-to-all-start.1
  84.7 1.8 pad_add_fusion
  86.5 76.8 %all_gather.7 = bf16[2048,128]{1,0:T(8,128)(2,1)} all-gather(bf16[64,128]{1,0:T(8,128)(2,1)S(1)} %bitcast.135), channel_id=1, replica_groups=mesh['seq'=32,'head'=8] {'seq'}, dimensions={0}, use_global_device_ids=true | all-gather | bytes 540672 | tf_op jit(solution)/shard_map/all_gather | solution.py:72
  163.3 3.8 collective-permute-start.1
  167.0 20.8 %all-to-all-start.5 = ((bf16[32,8,1024]{2,0,1:T(8,128)(2,1)}), bf16[32,8,1024]{2,0,1:T(8,128)(2,1)}, u32[]{:S(2)}, u32[]{:S(2)}) async-start(bf16[32,8,1024]{2,0,1:T(8,128)(2,1)} %bitcast.95), calls=%async_computation.5 | async-start | bytes 1048576 | tf_op jit(solution)/shard_map/all_to_all | solution.py:68
  187.8 73.2 %all_gather.6 = bf16[2048,128]{1,0:T(8,128)(2,1)S(1)} all-gather(bf16[64,128]{1,0:T(8,128)(2,1)S(1)} %bitcast.134), channel_id=1, replica_groups=mesh['seq'=32,'head'=8] {'seq'}, dimensions={0}, use_global_device_ids=true | all-gather | bytes 540672 | tf_op jit(solution)/shard_map/all_gather | solution.py:71
  265.5 2.1 maximum_select_fusion
  267.5 111.2 %while.17 = (s32[]{:T(128)}, f32[2560,128]{1,0:T(8,128)S(1)}, f32[2560,128]{1,0:T(8,128)S(1)}, bf16[8,320,128]{2,1,0:T(8,128)(2,1)}, bf16[8,320,128]{2,1,0:T(8,1...) while((s32[]{:T(128)}, f32[2560,128]{1,0:T(8,128)S(1)}, ...), condition=%wide.region_5.6_spmd.clone, body=%wide.region_1.5_spmd.clone.sunk | while | flops 1270865280 | bytes 33356120 | solution.py:121
  268.8 2.2 fusion.56
  273.9 2.3 convolution_add_fusion.2
  276.2 1.8 fusion.57
  279.2 2.2 fusion.58
  282.7 2.2 fusion.56
  287.8 2.3 convolution_add_fusion.2
  290.1 1.8 fusion.57
  293.1 2.2 fusion.58
  296.6 2.2 fusion.56
  301.7 2.3 convolution_add_fusion.2
  304.0 1.8 fusion.57
  307.0 2.2 fusion.58
  310.5 2.2 fusion.56
  315.6 2.3 convolution_add_fusion.2
  317.9 1.8 fusion.57
  320.9 2.2 fusion.58
  324.4 2.2 fusion.56
  329.5 2.3 convolution_add_fusion.2
  334.8 2.2 fusion.58
  338.3 2.2 fusion.56
  343.4 2.3 convolution_add_fusion.2
  345.7 1.8 fusion.57
  348.7 2.2 fusion.58
  352.2 2.2 fusion.56
  357.3 2.3 convolution_add_fusion.2
  362.6 2.2 fusion.58
  366.1 2.2 fusion.56
  371.2 2.3 convolution_add_fusion.2
  376.5 2.2 fusion.58
  380.8 153.0 %all-reduce.4 = (bf16[2048,128]{1,0:T(8,128)(2,1)}, bf16[2048,128]{1,0:T(8,128)(2,1)}) all-reduce(f32[2048,128]{1,0:T(8,128)} %slice.36, f32[2048,128]{1,0:T(8,128)} %slice.37), channel_id=1, replica_groups=mesh['seq'=32,'head'=8] {'seq'}, use_global_device_ids=true, to_apply=%region_6.7 | all-reduce | flops 524288 | bytes 3145728 | tf_op jit(solution)/shard_map/psum | solution.py:126
  535.1 49.1 %all-to-all-start.11 = ((bf16[8,8,128]{2,1,0:T(8,128)(2,1)}), bf16[8,8,128]{2,1,0:T(8,128)(2,1)S(1)}, u32[]{:S(2)}, u32[]{:S(2)}) async-start(bf16[8,8,128]{2,1,0:T(8,128)(2,1)} %fusion.19), calls=%async_computation.11 | async-start | bytes 32768 | tf_op jit(solution)/shard_map/all_to_all | solution.py:145
  585.5 5.7 all-to-all-done.11
  591.2 4.0 all-to-all-start.10
  596.9 5.4 all-to-all-done.10
  602.3 4.0 all-to-all-start.8
  614.3 5.5 all-to-all-start.9
  621.3 6.6 all-to-all-done.9
  627.9 4.5 all-to-all-start.15
  633.9 5.9 all-to-all-done.15
  639.9 4.0 all-to-all-start.14
  646.3 4.9 all-to-all-done.14
  651.2 4.3 all-to-all-start.12
  656.9 11.9 %all-to-all-done.12 = bf16[8,32,1024]{2,1,0:T(8,128)(2,1)S(1)} async-done(((bf16[8,32,1024]{2,1,0:T(8,128)(2,1)}), bf16[8,32,1024]{2,1,0:T(8,128)(2,1)S(1)}, u32[]{:S(2)}, u32[]{:S(2)}) %all-to-all-start.12) | async-done | bytes 524320 | tf_op jit(solution)/shard_map/all_to_all | solution.py:148
  668.9 5.7 all-to-all-start.13
  676.7 11.1 %all-to-all-done.13 = bf16[8,32,1024]{2,1,0:T(8,128)(2,1)S(1)} async-done(((bf16[8,32,1024]{2,1,0:T(8,128)(2,1)}), bf16[8,32,1024]{2,1,0:T(8,128)(2,1)S(1)}, u32[]{:S(2)}, u32[]{:S(2)}) %all-to-all-start.13) | async-done | bytes 524320 | tf_op jit(solution)/shard_map/all_to_all | solution.py:149
  (142 shorter events, 84.6 us)
Async XLA Ops:
  0.6 21.2 %copy-start = (bf16[32,1024]{1,0:T(8,128)(2,1)S(1)}, bf16[32,1024]{1,0:T(8,128)(2,1)}, u32[]{:S(2)}) copy-start(bf16[32,1024]{1,0:T(8,128)(2,1)} %param.17) | copy-start | bytes 196612
  0.6 71.9 %copy-start.6 = (bf16[32,8192]{1,0:T(8,128)(2,1)S(1)}, bf16[32,8192]{1,0:T(8,128)(2,1)}, u32[]{:S(2)}) copy-start(bf16[32,8192]{1,0:T(8,128)(2,1)} %param.19) | copy-start | bytes 1572868
  17.9 11.1 %all-to-all-start.6 = ((bf16[8,8,128]{2,0,1:T(8,128)(2,1)}), bf16[8,8,128]{2,0,1:T(8,128)(2,1)S(1)}, u32[]{:S(2)}, u32[]{:S(2)}) async-start(bf16[8,8,128]{2,0,1:T(8,128)(2,1)} %bitcast.139), calls=%async_computation.6 | async-start | bytes 32768 | tf_op jit(solution)/shard_map/all_to_all | solution.py:63
  28.9 0.6 copy-start.7
  29.5 11.6 %all-to-all-start.3 = ((bf16[32,8,128]{2,0,1:T(8,128)(2,1)}), bf16[32,8,128]{2,0,1:T(8,128)(2,1)S(1)}, u32[]{:S(2)}, u32[]{:S(2)}) async-start(bf16[32,8,128]{2,0,1:T(8,128)(2,1)} %copy_bitcast_fusion.5), calls=%async_computation.3 | async-start | bytes 131072 | tf_op jit(solution)/shard_map/all_to_all | solution.py:66
  52.2 12.4 %all-to-all-start = ((bf16[8,8,1024]{2,0,1:T(8,128)(2,1)}), bf16[8,8,1024]{2,0,1:T(8,128)(2,1)S(1)}, u32[]{:S(2)}, u32[]{:S(2)}) async-start(bf16[8,8,1024]{2,0,1:T(8,128)(2,1)} %bitcast.132), calls=%async_computation | async-start | bytes 262144 | tf_op jit(solution)/shard_map/all_to_all | solution.py:61
  64.6 12.9 %all-to-all-start.4 = ((bf16[8,8,1024]{2,0,1:T(8,128)(2,1)}), bf16[8,8,1024]{2,0,1:T(8,128)(2,1)S(1)}, u32[]{:S(2)}, u32[]{:S(2)}) async-start(bf16[8,8,1024]{2,0,1:T(8,128)(2,1)} %bitcast.133), calls=%async_computation.4 | async-start | bytes 262144 | tf_op jit(solution)/shard_map/all_to_all | solution.py:64
  77.5 0.7 copy-start.5
  78.2 88.8 %all-to-all-start.1 = ((bf16[32,8,1024]{2,0,1:T(8,128)(2,1)}), bf16[32,8,1024]{2,0,1:T(8,128)(2,1)S(1)}, u32[]{:S(2)}, u32[]{:S(2)}) async-start(bf16[32,8,1024]{2,0,1:T(8,128)(2,1)} %bitcast.116), calls=%async_computation.1 | async-start | bytes 1048576 | tf_op jit(solution)/shard_map/all_to_all | solution.py:65
  83.7 2.8 copy-start.8
  163.3 99.1 %collective-permute-start.1 = (bf16[256,128]{1,0:T(8,128)(2,1)}, bf16[256,128]{1,0:T(8,128)(2,1)}, u32[]{:S(2)}, u32[]{:S(2)}) collective-permute-start(bf16[256,128]{1,0:T(8,128)(2,1)} %bitcast.19), channel_id=1, source_target_pairs={{0,8},{8,16},{16,24},{24,32},{32,40},{40,48},{48,56},{56,64},{64,7... | collective-permute-start | bytes 196616 | tf_op jit(solution)/shard_map/ppermute | solution.py:14
  167.0 95.3 %copy-start.2 = (bf16[32,8,1024]{2,0,1:T(8,128)(2,1)}, bf16[32,8,1024]{2,0,1:T(8,128)(2,1)S(1)}, u32[]{:S(2)}) copy-start(bf16[32,8,1024]{2,0,1:T(8,128)(2,1)S(1)} %all-to-all-done.1) | copy-start | bytes 1572868
  167.0 98.4 %all-to-all-start.5 = ((bf16[32,8,1024]{2,0,1:T(8,128)(2,1)}), bf16[32,8,1024]{2,0,1:T(8,128)(2,1)}, u32[]{:S(2)}, u32[]{:S(2)}) async-start(bf16[32,8,1024]{2,0,1:T(8,128)(2,1)} %bitcast.95), calls=%async_computation.5 | async-start | bytes 1048576 | tf_op jit(solution)/shard_map/all_to_all | solution.py:68
  261.0 2.6 collective-permute-start
  262.4 2.2 copy-start.3
  263.6 1.9 copy-start.9
  276.2 1.8 copy-start.1
  290.1 1.8 copy-start.1
  304.0 1.8 copy-start.1
  317.9 1.8 copy-start.1
  331.8 1.8 copy-start.1
  345.7 1.8 copy-start.1
  359.6 1.8 copy-start.1
  373.5 1.8 copy-start.1
  380.8 228.1 %copy-start.4 = (bf16[8,320,128]{2,1,0:T(8,128)(2,1)S(1)}, bf16[8,320,128]{2,1,0:T(8,128)(2,1)}, u32[]{:S(2)}) copy-start(bf16[8,320,128]{2,1,0:T(8,128)(2,1)} %get-tuple-element.74) | copy-start | bytes 1966084
  535.1 56.1 %all-to-all-start.11 = ((bf16[8,8,128]{2,1,0:T(8,128)(2,1)}), bf16[8,8,128]{2,1,0:T(8,128)(2,1)S(1)}, u32[]{:S(2)}, u32[]{:S(2)}) async-start(bf16[8,8,128]{2,1,0:T(8,128)(2,1)} %fusion.19), calls=%async_computation.11 | async-start | bytes 32768 | tf_op jit(solution)/shard_map/all_to_all | solution.py:145
  591.2 11.0 %all-to-all-start.10 = ((bf16[8,8,128]{2,1,0:T(8,128)(2,1)}), bf16[8,8,128]{2,1,0:T(8,128)(2,1)S(1)}, u32[]{:S(2)}, u32[]{:S(2)}) async-start(bf16[8,8,128]{2,1,0:T(8,128)(2,1)} %fusion.18), calls=%async_computation.10 | async-start | bytes 32768 | tf_op jit(solution)/shard_map/all_to_all | solution.py:142
  602.3 12.0 %all-to-all-start.8 = ((bf16[8,8,1024]{2,1,0:T(8,128)(2,1)}), bf16[8,8,1024]{2,1,0:T(8,128)(2,1)S(1)}, u32[]{:S(2)}, u32[]{:S(2)}) async-start(bf16[8,8,1024]{2,1,0:T(8,128)(2,1)} %all_to_all.256), calls=%async_computation.8 | async-start | bytes 262144 | tf_op jit(solution)/shard_map/all_to_all | solution.py:140
  606.9 12.9 %collective-permute-start.3 = (f32[256,128]{1,0:T(8,128)}, f32[256,128]{1,0:T(8,128)}, u32[]{:S(2)}, u32[]{:S(2)}) collective-permute-start(f32[256,128]{1,0:T(8,128)} %slice.43), channel_id=1, source_target_pairs={{8,0},{16,8},{24,16},{32,24},{40,32},{48,40},{56,48},{64,56},{72,6... | collective-permute-start | bytes 393224 | tf_op jit(solution)/shard_map/ppermute | solution.py:14
  611.2 21.1 %collective-permute-start.2 = (f32[256,128]{1,0:T(8,128)}, f32[256,128]{1,0:T(8,128)}, u32[]{:S(2)}, u32[]{:S(2)}) collective-permute-start(f32[256,128]{1,0:T(8,128)} %slice.41), channel_id=1, source_target_pairs={{8,0},{16,8},{24,16},{32,24},{40,32},{48,40},{56,48},{64,56},{72,6... | collective-permute-start | bytes 393224 | tf_op jit(solution)/shard_map/ppermute | solution.py:14
  614.3 13.6 %all-to-all-start.9 = ((bf16[8,8,1024]{2,1,0:T(8,128)(2,1)}), bf16[8,8,1024]{2,1,0:T(8,128)(2,1)}, u32[]{:S(2)}, u32[]{:S(2)}) async-start(bf16[8,8,1024]{2,1,0:T(8,128)(2,1)} %all_to_all.260), calls=%async_computation.9 | async-start | bytes 262144 | tf_op jit(solution)/shard_map/all_to_all | solution.py:141
  627.9 11.9 %all-to-all-start.15 = ((bf16[8,32,128]{2,1,0:T(8,128)(2,1)}), bf16[8,32,128]{2,1,0:T(8,128)(2,1)S(1)}, u32[]{:S(2)}, u32[]{:S(2)}) async-start(bf16[8,32,128]{2,1,0:T(8,128)(2,1)} %bitcast.36), calls=%async_computation.15 | async-start | bytes 131072 | tf_op jit(solution)/shard_map/all_to_all | solution.py:151
  639.9 11.4 %all-to-all-start.14 = ((bf16[8,32,128]{2,1,0:T(8,128)(2,1)}), bf16[8,32,128]{2,1,0:T(8,128)(2,1)S(1)}, u32[]{:S(2)}, u32[]{:S(2)}) async-start(bf16[8,32,128]{2,1,0:T(8,128)(2,1)} %bitcast.34), calls=%async_computation.14 | async-start | bytes 131072 | tf_op jit(solution)/shard_map/all_to_all | solution.py:150
  651.2 17.6 %all-to-all-start.12 = ((bf16[8,32,1024]{2,1,0:T(8,128)(2,1)}), bf16[8,32,1024]{2,1,0:T(8,128)(2,1)S(1)}, u32[]{:S(2)}, u32[]{:S(2)}) async-start(bf16[8,32,1024]{2,1,0:T(8,128)(2,1)} %all_to_all.272), calls=%async_computation.12 | async-start | bytes 1048576 | tf_op jit(solution)/shard_map/all_to_all | solution.py:148
  668.9 18.9 %all-to-all-start.13 = ((bf16[8,32,1024]{2,1,0:T(8,128)(2,1)}), bf16[8,32,1024]{2,1,0:T(8,128)(2,1)S(1)}, u32[]{:S(2)}, u32[]{:S(2)}) async-start(bf16[8,32,1024]{2,1,0:T(8,128)(2,1)} %all_to_all.276), calls=%async_computation.13 | async-start | bytes 1048576 | tf_op jit(solution)/shard_map/all_to_all | solution.py:149
where the time goes:
time: 705 us; the launch traced here: 692 us
  blocking collectives  331 us (47%)
  starting transfers between devices  132 us (19%)
  matrix products  90.7 us (13%)
  waiting for transfers between devices  75 us (11%)
  local copies, waits for them, and re-layouts  37.1 us (5%)
  other arithmetic  19.4 us (3%)
    psum x1, blocking collectives, local(): lax.psum((acc_keys[:prompt_all], acc_values[:prompt_all]), 'seq')  153 us
    all_gather x1, blocking collectives, local(): lax.all_gather(prompt_value, 'seq', axis=0, tiled=True)  76.8 us
    all_gather x1, blocking collectives, local(): lax.all_gather(prompt_key, 'seq', axis=0, tiled=True)  73.2 us
    all_to_all x1, starting transfers between devices, local(): lax.all_to_all(prompt_value_grad.astype(jnp.bfloat16), 'head', split_axis...  49.1 us
    all_to_all x1, starting transfers between devices, local(): lax.all_to_all(cand_dout, 'head', split_axis=1, concat_axis=0, tiled=True)  20.8 us
    dot_general x8, matrix products, head_pass(): jnp.dot(weight_half.T, out_grads, preferred_element_type=jnp.float32)  18.6 us
    dot_general x8, matrix products, head_pass(): jnp.dot(queries, key_rows.T, preferred_element_type=jnp.float32) * scaling  17.7 us
    dot_general x8, matrix products, head_pass(): jnp.dot(grad_scores.T, queries, preferred_element_type=jnp.float32)  17.4 us
  transfers between devices with their start and end apart: 18, of which 13 were waited for; matrix products, arithmetic and copies ran while one was open for 4% of the time, Pallas kernels for 0%

commit v1 on v0

v1 whole, which is shorter than its diff:
```python
import functools
import math

import jax
import jax.numpy as jnp
from jax import lax
from jax.experimental import pallas as pl
from jax.experimental.pallas import tpu as pltpu
from jax.sharding import PartitionSpec as P

HD = 128
SCALE = 1.0 / math.sqrt(HD)
SCALE2 = SCALE * math.log2(math.e)
MESH = pl.DeviceIdType.MESH
f32, bf16 = jnp.float32, jnp.bfloat16
HIDDEN = -1e30


def coords():
    seq, head = lax.axis_index("seq"), lax.axis_index("head")
    x, y = seq % 4, (seq // 4) % 4
    z = (head // 2) * 2 + seq // 16
    return x, y, z, head % 2


def device(x, y, z, core):
    return ((z % 2) * 16 + y * 4 + x, (z // 2) * 2 + core)


def roles(x, y, core):
    xg, sx, yg, sy = x // 2, x % 2, y // 2, y % 2
    j = sy * 4 + sx * 2 + core
    g = ((sy + yg) % 2) * 4 + ((sx + xg) % 2) * 2 + core
    return xg, yg, j, g


def flip(value, bits):
    out = 0
    for bit in (4, 2, 1):
        digit = (value // bit) % 2
        out = out + bit * ((1 - digit) if bits & bit else digit)
    return out


def block_partner(x, y, z, core, d):
    px = x // 2 * 2 + (1 - x % 2 if d & 2 else x % 2)
    py = y // 2 * 2 + (1 - y % 2 if d & 4 else y % 2)
    return device(px, py, z, 1 - core if d & 1 else core)


def greet(partners):
    barrier = pltpu.get_barrier_semaphore()
    for partner in partners:
        pl.semaphore_signal(barrier, inc=1, device_id=partner, device_id_type=MESH)
    pl.semaphore_wait(barrier, len(partners))


def remote(src, dst, send, recv, target):
    return pltpu.make_async_remote_copy(
        src_ref=src, dst_ref=dst, send_sem=send, recv_sem=recv, device_id=target, device_id_type=MESH
    )


def gather_kernel(qd, kvp, kvc, qd_out, kvp_out, kvc_out, own, sends, recvs, psend, precv, csend, crecv):
    x, y, z, core = coords()
    xg, yg, j, g = roles(x, y, core)
    zhi = z // 2
    block = {d: block_partner(x, y, z, core, d) for d in range(1, 8)}
    mirror = (device(3 - x, y, z, core), device(x, 3 - y, z, core), device(3 - x, 3 - y, z, core))
    up, down = device(x, y, (z + 1) % 8, core), device(x, y, (z + 7) % 8, core)
    up2, down2 = device(x, y, (z + 2) % 8, core), device(x, y, (z + 6) % 8, core)
    greet(list(block.values()) + list(mirror) + [up, down, up2, down2])

    locals_ = [
        pltpu.make_async_copy(kvp.at[:, pl.ds(pl.multiple_of(g * 128, 128), 128)], kvp_out.at[z, yg, xg, j], own.at[0]),
        pltpu.make_async_copy(kvc.at[:, pl.ds(pl.multiple_of(g * 128, 128), 128)], kvc_out.at[zhi, j], own.at[1]),
        pltpu.make_async_copy(qd.at[:, pl.ds(pl.multiple_of(g * 1024, 1024), 1024)], qd_out.at[j], own.at[2]),
    ]
    for copy in locals_:
        copy.start()
    copies = {0: [], 1: [], 2: []}
    for kind in range(3):
        for d in range(1, 8):
            theirs = flip(g, d)
            if kind == 0:
                src, dst = kvp.at[:, pl.ds(pl.multiple_of(theirs * 128, 128), 128)], kvp_out.at[z, yg, xg, j]
            elif kind == 1:
                src, dst = kvc.at[:, pl.ds(pl.multiple_of(theirs * 128, 128), 128)], kvc_out.at[zhi, j]
            else:
                src, dst = qd.at[:, pl.ds(pl.multiple_of(theirs * 1024, 1024), 1024)], qd_out.at[j]
            copy = remote(src, dst, sends.at[kind, d], recvs.at[kind, d], block[d])
            copy.start()
            copies[kind].append(copy)

    locals_[0].wait()
    for copy in copies[0]:
        copy.wait()
    mirrored = [
        remote(kvp_out.at[z, yg, xg], kvp_out.at[z, yg, xg], psend.at[i], precv.at[i], mirror[i]) for i in range(3)
    ]
    for copy in mirrored:
        copy.start()
    locals_[1].wait()
    for copy in copies[1]:
        copy.wait()
    near = [
        remote(kvc_out.at[zhi], kvc_out.at[zhi], csend.at[0], crecv.at[0], up2),
        remote(kvc_out.at[zhi], kvc_out.at[zhi], csend.at[1], crecv.at[1], down2),
    ]
    for copy in mirrored:
        copy.wait()
    ring = []
    for step in range(3):
        rise, fall = (z + 8 - step) % 8, (z + step) % 8
        pair = [
            remote(kvp_out.at[rise], kvp_out.at[rise], psend.at[3 + step], precv.at[3 + step], up),
            remote(kvp_out.at[fall], kvp_out.at[fall], psend.at[7 + step], precv.at[7 + step], down),
        ]
        for copy in pair:
            copy.start()
        if step == 0:
            for copy in near:
                copy.start()
        for copy in pair:
            copy.wait()
    rise, fall = (z + 5) % 8, (z + 3) % 8
    last = [
        remote(kvp_out.at[rise, 0], kvp_out.at[rise, 0], psend.at[6], precv.at[6], up),
        remote(kvp_out.at[fall, 1], kvp_out.at[fall, 1], psend.at[10], precv.at[10], down),
    ]
    for copy in last:
        copy.start()
    for copy in near:
        copy.wait()
    below, above = (zhi + 3) % 4, (zhi + 1) % 4
    first, second = pl.ds(0, 4), pl.ds(4, 4)
    far = [
        remote(kvc_out.at[below, first], kvc_out.at[below, first], csend.at[2], crecv.at[2], up2),
        remote(kvc_out.at[above, second], kvc_out.at[above, second], csend.at[3], crecv.at[3], down2),
    ]
    for copy in far:
        copy.start()
    for copy in last + far:
        copy.wait()
    locals_[2].wait()
    for copy in copies[2]:
        copy.wait()


def nt(a, b):
    return lax.dot_general(a, b, (((1,), (1,)), ((), ())), preferred_element_type=f32)


def nn(a, b):
    return lax.dot_general(a, b, (((1,), (0,)), ((), ())), preferred_element_type=f32)


PART = 1024
PROMPT, SPAN = 2048, 512


def attend_kernel(
    meta, qd, kvp, kvc, od, dkvp, dkvc,
    kp, vp, kpt, vpt, ks, vs, kst, vst, scores, dkp, dvp, dks, dvs,
):
    z, yg, xg = meta[0], meta[1], meta[2]
    zhi = z // 2

    for i in range(8):
        both = kvp[i].reshape(32, 16, 128).astype(f32)
        rows = slice(i * 256, (i + 1) * 256)
        keys = both[:, 0:8, :].reshape(256, 128)
        values = both[:, 8:16, :].reshape(256, 128)
        kp[rows, :] = keys.astype(bf16)
        vp[rows, :] = values.astype(bf16)
        kpt[:, rows] = keys.T.astype(bf16)
        vpt[:, rows] = values.T.astype(bf16)
    for s in range(2):
        for half in range(2):
            for hi in range(4):
                for c in range(2):
                    at = half * 256 + hi * 64 + c * 32
                    ks[s, at : at + 32, :] = kvc[hi, s * 4 + half * 2 + c, 0:32, :]
                    vs[s, at : at + 32, :] = kvc[hi, s * 4 + half * 2 + c, 32:64, :]
        kst[s] = ks[s].astype(f32).T.astype(bf16)
        vst[s] = vs[s].astype(f32).T.astype(bf16)
    dkp[...] = jnp.zeros_like(dkp)
    dvp[...] = jnp.zeros_like(dvp)
    dks[...] = jnp.zeros_like(dks)
    dvs[...] = jnp.zeros_like(dvs)

    def tile(queries, grads, cand, row_at, live):
        peak = jnp.full((8, 256), HIDDEN, f32)
        for c in range(PROMPT // PART):
            rows = slice(c * PART, (c + 1) * PART)
            s = nt(kp[rows, :], queries)
            if not cand:
                n = c * PART + lax.broadcasted_iota(jnp.int32, (PART, 1), 0)
                zz = n // 256
                key_at = (
                    (zz % 2) * 1024 + (zz // 2) * 16
                    + ((n // 128) % 2) * 512 + ((n // 32) % 2) * 256
                    + ((n // 64) % 2) * 128 + ((n // 16) % 2) * 64
                    + ((n // 8) % 2) * 8 + n % 8
                )
                s = jnp.where(key_at <= row_at, s, HIDDEN)
            scores[rows, :] = s
            peak = jnp.maximum(peak, jnp.max(s.reshape(PART // 8, 8, 256), axis=0))
        parts = [slice(c * PART, (c + 1) * PART) for c in range(PROMPT // PART)]
        if cand:
            spans = []
            for i in range(2):
                lanes = slice(i * 128, (i + 1) * 128)
                s = nt(ks[i], queries[lanes, :])
                t = lax.broadcasted_iota(jnp.int32, (SPAN, 1), 0)
                s = jnp.where(t <= row_at[:, lanes], s, HIDDEN)
                scores[PROMPT:, lanes] = s
                spans.append(jnp.max(s.reshape(SPAN // 8, 8, 128), axis=0))
            peak = jnp.maximum(peak, jnp.concatenate(spans, axis=1))
            parts.append(slice(PROMPT, PROMPT + SPAN))
        peak = jnp.max(peak, axis=0, keepdims=True)
        total = jnp.zeros((8, 256), f32)
        for rows in parts:
            e = jnp.exp2((scores[rows, :] - peak) * SCALE2)
            scores[rows, :] = e
            total = total + jnp.sum(e.reshape(-1, 8, 256), axis=0)
        share = 1.0 / jnp.sum(total, axis=0, keepdims=True)
        out = jnp.zeros((128, 256), f32)
        for rows in parts[: PROMPT // PART]:
            half = (scores[rows, :] * share).astype(bf16)
            out = out + nn(vpt[:, rows], half)
            dvp[rows, :] += nn(half, grads)
        if cand:
            half = (scores[PROMPT:, :] * share).astype(bf16)
            spans = []
            for i in range(2):
                lanes = slice(i * 128, (i + 1) * 128)
                spans.append(nn(vst[i], half[:, lanes]))
                dvs[i] += nn(half[:, lanes], grads[lanes, :])
            out = out + jnp.concatenate(spans, axis=1)
            out = jnp.where(live, out, 0.0)
        delta = jnp.sum(out * grads.astype(f32).T, axis=0, keepdims=True)
        dq = jnp.zeros((128, 256), f32)
        for rows in parts[: PROMPT // PART]:
            dw = nt(vp[rows, :], grads)
            ds = (scores[rows, :] * share * (dw - delta)).astype(bf16)
            dq = dq + nn(kpt[:, rows], ds)
            dkp[rows, :] += nn(ds, queries)
        if cand:
            spans = []
            for i in range(2):
                lanes = slice(i * 128, (i + 1) * 128)
                dw = nt(vs[i], grads[lanes, :])
                ds = (scores[PROMPT:, lanes] * share[:, lanes] * (dw - delta[:, lanes])).astype(bf16)
                spans.append(nn(kst[i], ds))
                dks[i] += nn(ds, queries[lanes, :])
            dq = dq + jnp.concatenate(spans, axis=1)
        return out.T, (dq * SCALE).T

    lane = lax.broadcasted_iota(jnp.int32, (1, 256), 1)
    cand_at = ((lane // 64) % 2) * 256 + zhi * 64 + lane % 64
    live = cand_at < jnp.where(lane < 128, meta[3], meta[4])
    live_rows = [
        (half * 256 + zhi * 64 + lax.broadcasted_iota(jnp.int32, (64, 1), 0)) < meta[3 + s]
        for s in range(2)
        for half in range(2)
    ]
    live_rows = jnp.concatenate([m.astype(f32) for m in live_rows], axis=0) > 0.5

    def cand_head(h, carry):
        cols = pl.ds(pl.multiple_of(h * 128, 128), 128)
        queries = jnp.concatenate([qd[i, 0:32, cols] for i in range(8)], axis=0)
        grads = jnp.concatenate([qd[i, 32:64, cols] for i in range(8)], axis=0)
        grads = jnp.where(live_rows, grads.astype(f32), 0.0).astype(bf16)
        out, dq = tile(queries, grads, True, cand_at, live)
        for i in range(8):
            od[i, 0:32, cols] = out[i * 32 : (i + 1) * 32, :].astype(bf16)
            od[i, 32:64, cols] = dq[i * 32 : (i + 1) * 32, :].astype(bf16)
        return carry

    lax.fori_loop(0, 8, cand_head, 0)

    prompt_at = (
        (z % 2) * 1024 + (z // 2) * 16 + yg * 512 + xg * 128
        + ((lane // 32) % 2) * 256 + ((lane // 16) % 2) * 64 + ((lane // 8) % 2) * 8 + lane % 8
    )

    def prompt_heads(t, carry):
        queries, grads = [], []
        for h in range(4):
            cols = pl.ds(pl.multiple_of(t * 512 + h * 128, 128), 128)
            for i in range(8):
                both = qd[i, 64:80, cols].astype(f32)
                queries.append(both[0:8])
                grads.append(both[8:16])
        queries = jnp.concatenate(queries, axis=0).astype(bf16)
        grads = jnp.concatenate(grads, axis=0).astype(bf16)
        out, dq = tile(queries, grads, False, prompt_at, None)
        for h in range(4):
            cols = pl.ds(pl.multiple_of(t * 512 + h * 128, 128), 128)
            for i in range(8):
                at = h * 64 + i * 8
                both = jnp.concatenate([out[at : at + 8], dq[at : at + 8]], axis=0)
                od[i, 64:80, cols] = both.astype(bf16)
        return carry

    lax.fori_loop(0, 2, prompt_heads, 0)

    for i in range(8):
        rows = slice(i * 256, (i + 1) * 256)
        both = jnp.concatenate(
            [(dkp[rows, :] * SCALE).reshape(32, 8, 128), dvp[rows, :].reshape(32, 8, 128)], axis=1
        )
        dkvp[i] = both.astype(bf16).reshape(2, 2, 8, 16, 128)
    for s in range(2):
        for half in range(2):
            for hi in range(4):
                for c in range(2):
                    at = half * 256 + hi * 64 + c * 32
                    place = s * 4 + half * 2 + c
                    dkvc[hi, place, 0:32, :] = (dks[s, at : at + 32, :] * SCALE).astype(bf16)
                    dkvc[hi, place, 32:64, :] = dvs[s, at : at + 32, :].astype(bf16)


def scatter_kernel(
    od, dkvp, dkvc, od_out, kvp_out, kvc_out,
    rising, falling, rise_sum, fall_sum, zsum, mirrored_in, psum, cand_in, csum,
    own, sends, recvs, psend, precv, csend, crecv,
):
    x, y, z, core = coords()
    xg, yg, j, g = roles(x, y, core)
    zhi = z // 2
    block = {d: block_partner(x, y, z, core, d) for d in range(1, 8)}
    mirror = (device(3 - x, y, z, core), device(x, 3 - y, z, core), device(3 - x, 3 - y, z, core))
    up, down = device(x, y, (z + 1) % 8, core), device(x, y, (z + 7) % 8, core)
    hops = [device(x, y, (z + 2 * i) % 8, core) for i in (1, 3, 2)]
    greet(list(block.values()) + list(mirror) + [up, down] + hops)

    ring = [
        remote(dkvp.at[(z + 4) % 8, 0], rising.at[0, 0], psend.at[0], precv.at[0], up),
        remote(dkvp.at[(z + 4) % 8, 1], falling.at[0, 1], psend.at[4], precv.at[4], down),
    ]
    for copy in ring:
        copy.start()
    cand = [
        remote(dkvc.at[(zhi + i) % 4], cand_in.at[n], csend.at[n], crecv.at[n], hops[n])
        for n, i in enumerate((1, 3, 2))
    ]
    for copy in cand:
        copy.start()
    back = [pltpu.make_async_copy(od.at[j], od_out.at[:, pl.ds(pl.multiple_of(g * 1024, 1024), 1024)], own.at[0])]
    for d in range(1, 8):
        back.append(
            remote(
                od.at[flip(j, d)],
                od_out.at[:, pl.ds(pl.multiple_of(g * 1024, 1024), 1024)],
                sends.at[0, d], recvs.at[0, d], block[d],
            )
        )
    for copy in back:
        copy.start()
    for step in range(1, 4):
        for copy in ring:
            copy.wait()
        far_up, far_down = (z + 4 - step) % 8, (z + 4 + step) % 8
        if step == 1:
            rise_sum[0, 0] = (dkvp[far_up, 0].astype(f32) + rising[0, 0].astype(f32)).astype(bf16)
            rise_sum[0, 1] = dkvp[far_up, 1]
            fall_sum[0, 1] = (dkvp[far_down, 1].astype(f32) + falling[0, 1].astype(f32)).astype(bf16)
            fall_sum[0, 0] = dkvp[far_down, 0]
        else:
            rise_sum[step - 1] = (dkvp[far_up].astype(f32) + rising[step - 1].astype(f32)).astype(bf16)
            fall_sum[step - 1] = (dkvp[far_down].astype(f32) + falling[step - 1].astype(f32)).astype(bf16)
        ring = [
            remote(rise_sum.at[step - 1], rising.at[step], psend.at[step], precv.at[step], up),
            remote(fall_sum.at[step - 1], falling.at[step], psend.at[4 + step], precv.at[4 + step], down),
        ]
        for copy in ring:
            copy.start()
    for copy in cand:
        copy.wait()
    csum[...] = (
        dkvc[zhi].astype(f32) + cand_in[0].astype(f32) + cand_in[1].astype(f32) + cand_in[2].astype(f32)
    ).astype(bf16)
    cols = pl.ds(pl.multiple_of(g * 128, 128), 128)
    cand_back = [pltpu.make_async_copy(csum.at[j], kvc_out.at[:, cols], own.at[1])]
    for d in range(1, 8):
        cand_back.append(remote(csum.at[flip(j, d)], kvc_out.at[:, cols], sends.at[1, d], recvs.at[1, d], block[d]))
    for copy in cand_back:
        copy.start()
    for copy in ring:
        copy.wait()
    zsum[...] = (dkvp[z].astype(f32) + rising[3].astype(f32) + falling[3].astype(f32)).astype(bf16)
    across = [
        remote(zsum.at[yg, 1 - xg], mirrored_in.at[0], psend.at[8], precv.at[8], mirror[0]),
        remote(zsum.at[1 - yg, xg], mirrored_in.at[1], psend.at[9], precv.at[9], mirror[1]),
        remote(zsum.at[1 - yg, 1 - xg], mirrored_in.at[2], psend.at[10], precv.at[10], mirror[2]),
    ]
    for copy in across:
        copy.start()
    for copy in across:
        copy.wait()
    psum[...] = (
        zsum[yg, xg].astype(f32)
        + mirrored_in[0].astype(f32) + mirrored_in[1].astype(f32) + mirrored_in[2].astype(f32)
    ).astype(bf16)
    prompt_back = [pltpu.make_async_copy(psum.at[j], kvp_out.at[:, cols], own.at[2])]
    for d in range(1, 8):
        prompt_back.append(remote(psum.at[flip(j, d)], kvp_out.at[:, cols], sends.at[2, d], recvs.at[2, d], block[d]))
    for copy in prompt_back:
        copy.start()
    for copy in back + cand_back + prompt_back:
        copy.wait()


ANY = pl.BlockSpec(memory_space=pl.ANY)
VMEM = pl.BlockSpec(memory_space=pltpu.VMEM)
SMEM = pl.BlockSpec(memory_space=pltpu.SMEM)


def local(
    prompt_q, prompt_k, prompt_v, prompt_dout, cand_q, cand_k, cand_v, cand_dout, cand_len, placement
):
    x, y, z, core = coords()
    slots = (z % 2) * 8 + ((y // 2) * 2 + jnp.arange(2, dtype=jnp.int32)) * 2 + x // 2
    lengths = jnp.sum(jnp.where(placement[None, :] == slots[:, None], cand_len[None, :], 0), axis=1)
    meta = jnp.concatenate([jnp.stack([z, y // 2, x // 2]), lengths]).astype(jnp.int32)
    qd = jnp.concatenate([cand_q, cand_dout, prompt_q, prompt_dout], axis=0)
    kvp = jnp.concatenate([prompt_k, prompt_v], axis=0)
    kvc = jnp.concatenate([cand_k, cand_v], axis=0)
    DMA = pltpu.SemaphoreType.DMA
    qd_shape = jax.ShapeDtypeStruct((8, 80, 1024), bf16)
    kvp_shape = jax.ShapeDtypeStruct((8, 2, 2, 8, 16, 128), bf16)
    kvc_shape = jax.ShapeDtypeStruct((4, 8, 64, 128), bf16)
    qd, kvp, kvc = pl.pallas_call(
        gather_kernel,
        out_shape=(qd_shape, kvp_shape, kvc_shape),
        in_specs=[ANY] * 3,
        out_specs=(ANY,) * 3,
        scratch_shapes=[DMA((3,)), DMA((3, 8)), DMA((3, 8)), DMA((11,)), DMA((11,)), DMA((4,)), DMA((4,))],
        compiler_params=pltpu.CompilerParams(collective_id=0, has_side_effects=True),
        name="gather",
    )(qd, kvp, kvc)
    od, dkvp, dkvc = pl.pallas_call(
        attend_kernel,
        out_shape=(qd_shape, kvp_shape, kvc_shape),
        in_specs=[SMEM, VMEM, VMEM, VMEM],
        out_specs=(VMEM,) * 3,
        scratch_shapes=[
            pltpu.VMEM((PROMPT, 128), bf16), pltpu.VMEM((PROMPT, 128), bf16),
            pltpu.VMEM((128, PROMPT), bf16), pltpu.VMEM((128, PROMPT), bf16),
            pltpu.VMEM((2, SPAN, 128), bf16), pltpu.VMEM((2, SPAN, 128), bf16),
            pltpu.VMEM((2, 128, SPAN), bf16), pltpu.VMEM((2, 128, SPAN), bf16),
            pltpu.VMEM((PROMPT + SPAN, 256), f32),
            pltpu.VMEM((PROMPT, 128), f32), pltpu.VMEM((PROMPT, 128), f32),
            pltpu.VMEM((2, SPAN, 128), f32), pltpu.VMEM((2, SPAN, 128), f32),
        ],
        compiler_params=pltpu.CompilerParams(vmem_limit_bytes=48 * 2**20),
        name="attend",
    )(meta, qd, kvp, kvc)
    part = (2, 2, 8, 16, 128)
    od, dkvp, dkvc = pl.pallas_call(
        scatter_kernel,
        out_shape=(
            jax.ShapeDtypeStruct((80, 8192), bf16),
            jax.ShapeDtypeStruct((16, 1024), bf16),
            jax.ShapeDtypeStruct((64, 1024), bf16),
        ),
        in_specs=[ANY, VMEM, VMEM],
        out_specs=(ANY,) * 3,
        scratch_shapes=[
            pltpu.VMEM((4,) + part, bf16), pltpu.VMEM((4,) + part, bf16),
            pltpu.VMEM((3,) + part, bf16), pltpu.VMEM((3,) + part, bf16),
            pltpu.VMEM(part, bf16), pltpu.VMEM((3, 8, 16, 128), bf16), pltpu.VMEM((8, 16, 128), bf16),
            pltpu.VMEM((3, 8, 64, 128), bf16), pltpu.VMEM((8, 64, 128), bf16),
            DMA((3,)), DMA((3, 8)), DMA((3, 8)), DMA((11,)), DMA((11,)), DMA((3,)), DMA((3,)),
        ],
        compiler_params=pltpu.CompilerParams(
            collective_id=1, has_side_effects=True, vmem_limit_bytes=24 * 2**20
        ),
        name="scatter",
    )(od, dkvp, dkvc)
    return (
        od[64:72], od[72:80], dkvp[0:8], dkvp[8:16],
        od[0:32], od[32:64], dkvc[0:32], dkvc[32:64],
    )


def solution(mesh):
    rows = P(("seq", "head"), None)
    return jax.shard_map(
        local,
        mesh=mesh,
        in_specs=(rows,) * 8 + (P(), P()),
        out_specs=(rows,) * 8,
        check_vma=False,
    )
```

time: 705 us -> 128 us (0.18); the launches traced: 692 us -> 127 us
  blocking collectives: 331 us -> 0 us
  starting transfers between devices: 132 us -> 0 us
  Pallas kernels: 0 us -> 114 us
  matrix products: 90.7 us -> 0 us
  waiting for transfers between devices: 75 us -> 0 us
  local copies, waits for them, and re-layouts: 37.1 us -> 6.6 us
  other arithmetic: 19.4 us -> 6.33 us
    psum x1 -> x0, blocking collectives: 153 us -> none  [local(): lax.psum((acc_keys[:prompt_all], acc_values[:prompt_all]), 'seq')]
    all_gather x2 -> x0, blocking collectives: 150 us -> none  [the longest x1 76.8 us: local(): lax.all_gather(prompt_value, 'seq', axis=0, tiled=True)]
    all_to_all x14 -> x0, starting transfers between devices: 124 us -> none  [the longest x1 49.1 us: local(): lax.all_to_all(prompt_value_grad.astype(jnp.bfloat16), 'head', split_axis...]
    pallas_call x0 -> x3, Pallas kernels: none -> 114 us  [the longest x1 40 us: local(): pl.pallas_call(scatter_kernel, out_shape=(jax.ShapeDtypeStruct((80, 8192)...]
    dot_general x48 -> x0, matrix products: 90.7 us -> none  [the longest x8 18.6 us: head_pass(): jnp.dot(weight_half.T, out_grads, preferred_element_type=jnp.float32)]
    all_to_all x14 -> x0, waiting for transfers between devices: 75 us -> none  [the longest x1 11.9 us: local(): lax.all_to_all(outputs[prompt_dev:], 'head', split_axis=0, concat_axis=1,...]
    all_to_all x2 -> x0, blocking collectives: 28.3 us -> none  [the longest x1 17.2 us: local(): lax.all_to_all(prompt_k, 'head', split_axis=1, concat_axis=0, tiled=True)]
    all_to_all x14 -> x0, local copies, waits for them, and re-layouts: 14.2 us -> none  [the longest x1 1.87 us: local(): lax.all_to_all(cand_q, 'head', split_axis=1, concat_axis=0, tiled=True)]
  transfers between devices with their start and end apart: 18 -> 0, of which waited for: 13 -> 0; matrix products, arithmetic and copies ran while one was open for 4% -> 0% of each run, Pallas kernels for 0% -> 0%
where the time goes in v1:
time: 128 us; the launch traced here: 127 us
  Pallas kernels  114 us (89%)
  local copies, waits for them, and re-layouts  6.6 us (5%)
  other arithmetic  6.33 us (5%)
    pallas_call x1, Pallas kernels, local(): pl.pallas_call(scatter_kernel, out_shape=(jax.ShapeDtypeStruct((80, 8192)...  40 us
    pallas_call x1, Pallas kernels, local(): pl.pallas_call(gather_kernel, out_shape=(qd_shape, kvp_shape, kvc_shape),...  39.8 us
    pallas_call x1, Pallas kernels, local(): pl.pallas_call(attend_kernel, out_shape=(qd_shape, kvp_shape, kvc_shape),...  33.9 us
    unnamed x6, local copies, waits for them, and re-layouts  3.57 us

profile of v1, /device:TPU:1, one launch (start us, length us, event | category | flops | bytes accessed | tf_op | source)
XLA Modules:
  0.0 127.3 jit_solution(15231649052601872985)
XLA Ops:
  0.8 0.9 fusion
  1.6 0.1 pad_add_fusion.meta
  1.7 1.4 %pad_maximum_fusion.2.kvp = bf16[16,1024]{1,0:T(8,128)(2,1)} fusion(bf16[8,1024]{1,0:T(8,128)(2,1)} %param.12, bf16[8,1024]{1,0:T(8,128)(2,1)} %param.11), kind=kLoop, calls=%fused_computation.2 | loop fusion | flops 65536 | bytes 65536 | tf_op jit(solution)/shard_map/concatenate | solution.py:429
  3.0 1.5 %pad_maximum_fusion.1.kvc = bf16[64,1024]{1,0:T(8,128)(2,1)} fusion(bf16[32,1024]{1,0:T(8,128)(2,1)} %param.16, bf16[32,1024]{1,0:T(8,128)(2,1)} %param.15), kind=kLoop, calls=%fused_computation.1 | loop fusion | flops 262144 | bytes 262144 | tf_op jit(solution)/shard_map/concatenate | solution.py:430
  4.6 2.5 %pad_maximum_fusion.qd = bf16[80,8192]{1,0:T(8,128)(2,1)} fusion(bf16[8,8192]{1,0:T(8,128)(2,1)} %param.13, bf16[8,8192]{1,0:T(8,128)(2,1)} %param.10, bf16[32,8192]{1,0:T(8,128)(2,1)} %param.17, bf16[32,8192]{1,0:T(8,128)(2,1)} %param.14), kind=kLoop, calls=%fused_computation | loop fusion | flops 5242880 | bytes 2621440 | tf_op jit(solution)/shard_map/concatenate | solution.py:428
  7.1 39.8 %gather.1 = (bf16[8,80,1024]{2,1,0:T(8,128)(2,1)}, bf16[8,2,2,8,16,128]{5,4,3,2,1,0:T(8,128)(2,1)}, bf16[4,8,64,128]{3,2,1,0:T(8,128)(2,1)}) custom-call(bf16[80,8192]{1,0:T(8,128)(2,1)} %pad_maximum_fusion.qd, bf16[16,1024]{1,0:T(8,128)(2,1)} %pad_maximum_fusion.2.kvp, bf16[64,1024]{1,0:T(8,128)(2,1)} %pad_maximum_fusion.1.kvc), custom_call_target="tpu_custom_call" | custom-call | tf_op jit(solution)/shard_map/gather/pallas_call | solution.py:435
  46.9 0.0 copy-start
  46.9 1.3 %copy-done = bf16[8,80,1024]{2,1,0:T(8,128)(2,1)S(1)} copy-done((bf16[8,80,1024]{2,1,0:T(8,128)(2,1)S(1)}, bf16[8,80,1024]{2,1,0:T(8,128)(2,1)}, u32[]{:S(2)}) %copy-start) | copy-done | bytes 1310744
  48.2 0.0 copy-start.1
  48.2 1.2 copy-done.1
  49.4 0.0 copy-start.2
  49.4 1.0 copy-done.2
  50.4 33.9 %attend.1 = (bf16[8,80,1024]{2,1,0:T(8,128)(2,1)S(1)}, bf16[8,2,2,8,16,128]{5,4,3,2,1,0:T(8,128)(2,1)S(1)}, bf16[4,8,64,128]{3,2,1,0:T(8,128)(2,1)S(1)}) custom-call(s32[5]{0:T(128)S(1)} %pad_add_fusion.meta, bf16[8,80,1024]{2,1,0:T(8,128)(2,1)S(1)} %copy-done, bf16[8,2,2,8,16,128]{5,4,3,2,1,0:T(8,128)(2,1)S(1)} %copy-done.1, ...), custom_call_target="tpu_custom_call" | custom-call | tf_op jit(solution)/shard_map/attend/pallas_call | solution.py:444
  84.3 40.0 %scatter.1 = (bf16[80,8192]{1,0:T(8,128)(2,1)S(1)}, bf16[16,1024]{1,0:T(8,128)(2,1)S(1)}, bf16[64,1024]{1,0:T(8,128)(2,1)S(1)}) custom-call(bf16[8,80,1024]{2,1,0:T(8,128)(2,1)S(1)} %get-tuple-element.20.od, bf16[8,2,2,8,16,128]{5,4,3,2,1,0:T(8,128)(2,1)S(1)} %get-tuple-element.21.dkvp, bf16[4,8,64,128]{3,2,1,0:T(8,128)(2,1)S(1)} %get-tuple-element.22.dkvc), custom_call_target="tpu_custom_call" | custom-call | tf_op jit(solution)/shard_map/scatter/pallas_call | solution.py:462
  124.3 0.6 fusion.4
  124.9 0.7 fusion.3
  125.5 0.7 fusion.2
  126.3 1.0 fusion.1
  (1 shorter events, 0.0 us)
Async XLA Ops:
  46.9 1.3 %copy-start = (bf16[8,80,1024]{2,1,0:T(8,128)(2,1)S(1)}, bf16[8,80,1024]{2,1,0:T(8,128)(2,1)}, u32[]{:S(2)}) copy-start(bf16[8,80,1024]{2,1,0:T(8,128)(2,1)} %get-tuple-element.17.qd) | copy-start | bytes 3932164
  48.2 1.2 copy-start.1
  49.4 1.0 copy-start.2

commit v2 on v0

v2 whole, which is shorter than its diff:
```python
import functools
import math

import jax
import jax.numpy as jnp
from jax import lax
from jax.experimental import pallas as pl
from jax.experimental.pallas import tpu as pltpu
from jax.sharding import PartitionSpec as P

HD = 128
SCALE = 1.0 / math.sqrt(HD)
SCALE2 = SCALE * math.log2(math.e)
MESH = pl.DeviceIdType.MESH
f32, bf16 = jnp.float32, jnp.bfloat16
HIDDEN = -1e30
PART = 512
PROMPT, SPAN = 2048, 512
KEYS = PROMPT + SPAN
LANES = 2560


def coords():
    seq, head = lax.axis_index("seq"), lax.axis_index("head")
    x, y = seq % 4, (seq // 4) % 4
    z = (head // 2) * 2 + seq // 16
    return x, y, z, head % 2


def device(x, y, z, core):
    return ((z % 2) * 16 + y * 4 + x, (z // 2) * 2 + core)


def roles(x, y, core):
    xg, sx, yg, sy = x // 2, x % 2, y // 2, y % 2
    j = sy * 4 + sx * 2 + core
    g = ((sy + yg) % 2) * 4 + ((sx + xg) % 2) * 2 + core
    return xg, yg, j, g


def flip(value, bits):
    out = 0
    for bit in (4, 2, 1):
        digit = (value // bit) % 2
        out = out + bit * ((1 - digit) if bits & bit else digit)
    return out


def block_partner(x, y, z, core, d):
    px = x // 2 * 2 + (1 - x % 2 if d & 2 else x % 2)
    py = y // 2 * 2 + (1 - y % 2 if d & 4 else y % 2)
    return device(px, py, z, 1 - core if d & 1 else core)


def greet(partners):
    barrier = pltpu.get_barrier_semaphore()
    for partner in partners:
        pl.semaphore_signal(barrier, inc=1, device_id=partner, device_id_type=MESH)
    pl.semaphore_wait(barrier, len(partners))


def remote(src, dst, send, recv, target):
    return pltpu.make_async_remote_copy(
        src_ref=src, dst_ref=dst, send_sem=send, recv_sem=recv, device_id=target, device_id_type=MESH
    )


def start(copies):
    for copy in copies:
        copy.start()


def wait(copies):
    for copy in copies:
        copy.wait()


def nt(a, b):
    return lax.dot_general(a, b, (((1,), (1,)), ((), ())), preferred_element_type=f32)


def nn(a, b):
    return lax.dot_general(a, b, (((1,), (0,)), ((), ())), preferred_element_type=f32)


def columns(index, width):
    return pl.ds(pl.multiple_of(index * width, width), width)


def kernel(
    cand_len, placement,
    prompt_q, prompt_k, prompt_v, prompt_dout, cand_q, cand_k, cand_v, cand_dout,
    oc_out, dqc_out, pp_out, kvp_out, ck_out, cv_out,
    pp_stage, kv_stage, kvp_in, kc, vc, qc_in, pp_in, gc_in, kq, vq,
    q_all, g_all, ks, vs, kpt, vpt, kst, vst,
    scores, halves, peaks, shares, deltas, prompt_out,
    oc, dqc, pp, dvb, dkb, rv, rk, zv, zk, zv_in, zk_in, dvown, dkown, vsum,
    dvc, dkc, cv_in, ck_in, cv_sum, ck_sum, psum,
    own, asend, arecv, zsend, zrecv, msend, mrecv, csend, crecv, bsend, brecv,
):
    x, y, z, core = coords()
    xg, yg, j, g = roles(x, y, core)
    zhi, sy = z // 2, y % 2
    block = {d: block_partner(x, y, z, core, d) for d in range(1, 8)}
    mirror = {
        1: device(3 - x, y, z, core), 2: device(x, 3 - y, z, core), 3: device(3 - x, 3 - y, z, core)
    }
    column = {d: device(x, y, (z + d) % 8, core) for d in range(1, 8)}

    both = jnp.concatenate([prompt_k[...].astype(f32), prompt_v[...].astype(f32)], axis=0)
    kv_stage[...] = both.astype(bf16)
    both = jnp.concatenate([prompt_q[...].astype(f32), prompt_dout[...].astype(f32)], axis=0)
    pp_stage[...] = both.astype(bf16)

    greet(list(block.values()) + list(mirror.values()) + list(column.values()))

    def exchange(kind, source, width, target):
        copies = [pltpu.make_async_copy(source.at[:, columns(g, width)], target, own.at[kind])]
        for d in range(1, 8):
            copies.append(
                remote(
                    source.at[:, columns(flip(g, d), width)], target,
                    asend.at[kind, d], arecv.at[kind, d], block[d],
                )
            )
        start(copies)
        return copies

    kvp_moves = exchange(0, kv_stage, 128, kvp_in.at[j])
    kc_moves = exchange(1, cand_k, 128, kc.at[zhi, j])
    q_moves = exchange(2, cand_q, 1024, qc_in.at[j])
    pp_moves = exchange(3, pp_stage, 1024, pp_in.at[j])
    vc_moves = exchange(4, cand_v, 128, vc.at[zhi, j])
    g_moves = exchange(5, cand_dout, 1024, gc_in.at[j])

    wait(kvp_moves)
    both = kvp_in[...].astype(f32)
    kq[0, z] = both[:, 0:8, :].reshape(64, 128).astype(bf16)
    vq[0, z] = both[:, 8:16, :].reshape(64, 128).astype(bf16)
    kz = [remote(kq.at[0, z], kq.at[0, z], zsend.at[0, d], zrecv.at[0, d], column[d]) for d in range(1, 8)]
    vz = [remote(vq.at[0, z], vq.at[0, z], zsend.at[1, d], zrecv.at[1, d], column[d]) for d in range(1, 8)]
    start(kz)
    wait(kc_moves)
    kc_near = [
        remote(kc.at[zhi], kc.at[zhi], csend.at[0], crecv.at[0], column[2]),
        remote(kc.at[zhi], kc.at[zhi], csend.at[1], crecv.at[1], column[6]),
    ]
    start(kc_near)
    start(vz)
    wait(kz)
    kquads = [remote(kq.at[0], kq.at[p], msend.at[0, p], mrecv.at[0, p], mirror[p]) for p in (1, 2, 3)]
    start(kquads)
    below, above = (zhi + 3) % 4, (zhi + 1) % 4
    first, second = pl.ds(0, 4), pl.ds(4, 4)
    wait(kc_near)
    kc_far = [
        remote(kc.at[below, first], kc.at[below, first], csend.at[2], crecv.at[2], column[2]),
        remote(kc.at[above, second], kc.at[above, second], csend.at[3], crecv.at[3], column[6]),
    ]
    start(kc_far)
    wait(vc_moves)
    vc_near = [
        remote(vc.at[zhi], vc.at[zhi], csend.at[4], crecv.at[4], column[2]),
        remote(vc.at[zhi], vc.at[zhi], csend.at[5], crecv.at[5], column[6]),
    ]
    start(vc_near)
    wait(vz)
    vquads = [remote(vq.at[0], vq.at[p], msend.at[1, p], mrecv.at[1, p], mirror[p]) for p in (1, 2, 3)]
    start(vquads)

    slots = (1 - sy, sy)
    wait(q_moves)
    for i in range(2):
        for k in range(4):
            rows = qc_in[slots[i] * 4 + k]
            for h in range(8):
                at = i * 1024 + h * 128 + k * 32
                q_all[at : at + 32, :] = rows[:, h * 128 : (h + 1) * 128]
    wait(pp_moves)
    for h in range(8):
        both = pp_in[:, :, h * 128 : (h + 1) * 128].astype(f32)
        at = 2048 + h * 64
        q_all[at : at + 64, :] = both[:, 0:8, :].reshape(64, 128).astype(bf16)
        g_all[at : at + 64, :] = both[:, 8:16, :].reshape(64, 128).astype(bf16)

    peaks[...] = jnp.full(peaks.shape, HIDDEN, f32)
    lane = lax.broadcasted_iota(jnp.int32, (1, 256), 1)
    cand_at = ((lane // 64) % 2) * 256 + zhi * 64 + lane % 64
    prompt_at = (
        (z % 2) * 1024 + zhi * 16 + yg * 512 + xg * 128
        + ((lane // 32) % 2) * 256 + ((lane // 16) % 2) * 64 + ((lane // 8) % 2) * 8 + lane % 8
    )

    def top(s):
        return jnp.max(s.reshape(-1, 8, 256), axis=0)

    def score_part(p):
        rows = slice(p * PART, (p + 1) * PART)
        keys = kq[p].reshape(PART, 128)

        def cand(t, carry):
            at = columns(t, 256)
            s = nt(keys, q_all[at, :])
            scores[rows, at] = s
            peaks[:, at] = jnp.maximum(peaks[:, at], top(s))
            return carry

        lax.fori_loop(0, 8, cand, 0)
        n = lax.broadcasted_iota(jnp.int32, (PART, 1), 0)
        zz = n // 64
        ygp = yg if p < 2 else 1 - yg
        xgp = xg if p % 2 == 0 else 1 - xg
        key_at = (
            (zz % 2) * 1024 + (zz // 2) * 16 + ygp * 512 + ((n // 32) % 2) * 256
            + xgp * 128 + ((n // 16) % 2) * 64 + ((n // 8) % 2) * 8 + n % 8
        )

        def prompt(t, carry):
            at = columns(t, 256)
            s = jnp.where(key_at <= prompt_at, nt(keys, q_all[at, :]), HIDDEN)
            scores[rows, at] = s
            peaks[:, at] = jnp.maximum(peaks[:, at], top(s))
            return carry

        lax.fori_loop(8, 10, prompt, 0)
        kpt[:, rows] = keys.astype(f32).T.astype(bf16)

    score_part(0)
    for p in (1, 2, 3):
        wait([kquads[p - 1]])
        score_part(p)

    def slot_rows(source, target, turned):
        for i in range(2):
            for half in range(2):
                for hi in range(4):
                    for c in range(2):
                        at = half * 256 + hi * 64 + c * 32
                        target[i, at : at + 32, :] = source[hi, slots[i] * 4 + half * 2 + c]
            turned[i] = target[i].astype(f32).T.astype(bf16)

    wait(vc_near)
    vc_far = [
        remote(vc.at[below, first], vc.at[below, first], csend.at[6], crecv.at[6], column[2]),
        remote(vc.at[above, second], vc.at[above, second], csend.at[7], crecv.at[7], column[6]),
    ]
    start(vc_far)
    wait(kc_far)
    slot_rows(kc, ks, kst)
    span_at = lax.broadcasted_iota(jnp.int32, (SPAN, 1), 0)

    def score_slot(t, carry):
        at = columns(t, 256)
        s = jnp.where(span_at <= cand_at, nt(ks[t // 4], q_all[at, :]), HIDDEN)
        scores[PROMPT:, at] = s
        peaks[:, at] = jnp.maximum(peaks[:, at], top(s))
        return carry

    lax.fori_loop(0, 8, score_slot, 0)

    lengths = []
    for i in range(2):
        slot = (z % 2) * 8 + ((y // 2) * 2 + slots[i]) * 2 + x // 2
        length = jnp.int32(0)
        for c in range(16):
            length = length + jnp.where(placement[c] == slot, cand_len[c], 0)
        lengths.append(length)
    wait(g_moves)
    row = lax.broadcasted_iota(jnp.int32, (32, 1), 0)
    for i in range(2):
        for k in range(4):
            kept = (k // 2) * 256 + zhi * 64 + (k % 2) * 32 + row < lengths[i]
            rows = jnp.where(kept, gc_in[slots[i] * 4 + k].astype(f32), 0.0).astype(bf16)
            for h in range(8):
                at = i * 1024 + h * 128 + k * 32
                g_all[at : at + 32, :] = rows[:, h * 128 : (h + 1) * 128]
    wait(vquads)
    for p in range(4):
        vpt[:, p * PART : (p + 1) * PART] = vq[p].reshape(PART, 128).astype(f32).T.astype(bf16)
    wait(vc_far)
    slot_rows(vc, vs, vst)

    def weigh(t, cand, i):
        at = columns(t, 256)
        parts = KEYS // PART if cand else PROMPT // PART
        peak = jnp.max(peaks[:, at], axis=0, keepdims=True)
        total = jnp.zeros((8, 256), f32)
        for p in range(parts):
            rows = slice(p * PART, (p + 1) * PART)
            e = jnp.exp2((scores[rows, at] - peak) * SCALE2)
            scores[rows, at] = e
            total = total + jnp.sum(e.reshape(-1, 8, 256), axis=0)
        share = 1.0 / jnp.sum(total, axis=0, keepdims=True)
        shares[:, at] = jnp.broadcast_to(share, (8, 256))
        for p in range(parts):
            rows = slice(p * PART, (p + 1) * PART)
            halves[rows, at] = (scores[rows, at] * share).astype(bf16)
        out = nn(vpt[...], halves[0:PROMPT, at])
        if cand:
            out = out + nn(vst[i], halves[PROMPT:, at])
            out = jnp.where(cand_at < lengths[i], out, 0.0)
        delta = jnp.sum(out * g_all[at, :].astype(f32).T, axis=0, keepdims=True)
        deltas[:, at] = jnp.broadcast_to(delta, (8, 256))
        return out.T

    def put_cand(target, i, pair, rows):
        for a in range(2):
            for k in range(4):
                at = a * 128 + k * 32
                target[slots[i] * 4 + k, :, columns(pair * 2 + a, 128)] = rows[at : at + 32, :].astype(bf16)

    def give_back(kind, source, target, which):
        copies = []
        if 0 in which:
            copies.append(pltpu.make_async_copy(source.at[j], target, own.at[6 + kind]))
        for d in which:
            if d:
                copies.append(remote(source.at[flip(j, d)], target, bsend.at[kind, d], brecv.at[kind, d], block[d]))
        start(copies)
        return copies

    OTHER, OWN = (4, 5, 6, 7), (1, 2, 3, 0)
    back = []
    for i, which in enumerate((OTHER, OWN)):

        def weigh_cand(pair, carry, i=i):
            put_cand(oc, i, pair, weigh(i * 4 + pair, True, i))
            return carry

        lax.fori_loop(0, 4, weigh_cand, 0)
        back += give_back(0, oc, oc_out.at[:, columns(g, 1024)], which)

    def weigh_prompt(t, carry):
        prompt_out[columns(t, 256), :] = weigh(8 + t, False, None)
        return carry

    lax.fori_loop(0, 2, weigh_prompt, 0)

    def cand_terms(sums, target, i):
        for half in range(2):
            for hi in range(4):
                for c in range(2):
                    at = half * 256 + hi * 64 + c * 32
                    target[hi, slots[i] * 4 + half * 2 + c] = sums[at : at + 32, :].astype(bf16)

    def terms(others, scale, boxes, mine, inbox, kind, cand_box, cand_inbox):
        for i in range(2):
            rows = slice(i * 1024, (i + 1) * 1024)
            cand_terms(nn(halves[PROMPT:, rows], others[rows, :]) * scale, cand_box, i)
        cand_moves = [
            remote(
                cand_box.at[(zhi + n) % 4], cand_inbox.at[n - 1],
                csend.at[8 + kind * 3 + n - 1], crecv.at[8 + kind * 3 + n - 1], column[2 * n],
            )
            for n in (1, 2, 3)
        ]
        start(cand_moves)
        moves = []
        for p in (3, 1, 2, 0):
            total = nn(halves[p * PART : (p + 1) * PART, :], others[...]) * scale
            if p:
                boxes[p - 1] = total.reshape(8, 64, 128).astype(bf16)
                moves.append(
                    remote(boxes.at[p - 1], inbox.at[p - 1], msend.at[2 + kind, p], mrecv.at[2 + kind, p], mirror[p])
                )
                start(moves[-1:])
            else:
                mine[...] = total.reshape(8, 64, 128)
        return cand_moves, moves

    def along_z(mine, inbox, moves, stage, landed, kind):
        wait(moves)
        total = mine[...] + inbox[0].astype(f32) + inbox[1].astype(f32) + inbox[2].astype(f32)
        stage[...] = total.astype(bf16)
        hops = [
            remote(stage.at[(z + d) % 8], landed.at[d - 1], zsend.at[2 + kind, d], zrecv.at[2 + kind, d], column[d])
            for d in range(1, 8)
        ]
        start(hops)
        return hops

    def final(stage, landed, hops):
        wait(hops)
        total = stage[z].astype(f32)
        for d in range(7):
            total = total + landed[d].astype(f32)
        return total

    def cand_final(box, inbox, moves, total):
        wait(moves)
        total[...] = (
            box[zhi].astype(f32) + inbox[0].astype(f32) + inbox[1].astype(f32) + inbox[2].astype(f32)
        ).astype(bf16)

    vcand_moves, v_moves = terms(g_all, 1.0, dvb, dvown, rv, 0, dvc, cv_in)

    def grade(t, cand, i):
        at = columns(t, 256)
        grads = g_all[at, :]
        share, delta = shares[0:1, at], deltas[0:1, at]
        for p in range(PROMPT // PART):
            rows = slice(p * PART, (p + 1) * PART)
            dw = nt(vq[p].reshape(PART, 128), grads)
            halves[rows, at] = (scores[rows, at] * share * (dw - delta)).astype(bf16)
        dq = nn(kpt[...], halves[0:PROMPT, at])
        if cand:
            dw = nt(vs[i], grads)
            halves[PROMPT:, at] = (scores[PROMPT:, at] * share * (dw - delta)).astype(bf16)
            dq = dq + nn(kst[i], halves[PROMPT:, at])
        return (dq * SCALE).T

    def grade_prompt(t, carry):
        dq = grade(8 + t, False, None)
        out = prompt_out[columns(t, 256), :]
        for h in range(4):
            rows = slice(h * 64, (h + 1) * 64)
            both = jnp.concatenate([out[rows].reshape(8, 8, 128), dq[rows].reshape(8, 8, 128)], axis=1)
            pp[:, :, columns(t * 4 + h, 128)] = both.astype(bf16)
        return carry

    lax.fori_loop(0, 2, grade_prompt, 0)
    back += give_back(1, pp, pp_out.at[:, columns(g, 1024)], OTHER + OWN)
    for i, which in enumerate((OTHER, OWN)):

        def grade_cand(pair, carry, i=i):
            put_cand(dqc, i, pair, grade(i * 4 + pair, True, i))
            return carry

        lax.fori_loop(0, 4, grade_cand, 0)
        back += give_back(2, dqc, dqc_out.at[:, columns(g, 1024)], which)
        if i == 0:
            v_hops = along_z(dvown, rv, v_moves, zv, zv_in, 0)
            cand_final(dvc, cv_in, vcand_moves, cv_sum)
            back += give_back(3, cv_sum, cv_out.at[:, columns(g, 128)], OTHER + OWN)

    kcand_moves, k_moves = terms(q_all, SCALE, dkb, dkown, rk, 1, dkc, ck_in)
    k_hops = along_z(dkown, rk, k_moves, zk, zk_in, 1)
    vsum[...] = final(zv, zv_in, v_hops)
    cand_final(dkc, ck_in, kcand_moves, ck_sum)
    back += give_back(4, ck_sum, ck_out.at[:, columns(g, 128)], OTHER + OWN)
    ksum = final(zk, zk_in, k_hops)
    both = jnp.concatenate([ksum.reshape(8, 8, 128), vsum[...].reshape(8, 8, 128)], axis=1)
    psum[...] = both.astype(bf16)
    back += give_back(5, psum, kvp_out.at[:, columns(g, 128)], OTHER + OWN)
    wait(back)


ANY = pl.BlockSpec(memory_space=pl.ANY)
VMEM = pl.BlockSpec(memory_space=pltpu.VMEM)
SMEM = pl.BlockSpec(memory_space=pltpu.SMEM)


def local(
    prompt_q, prompt_k, prompt_v, prompt_dout, cand_q, cand_k, cand_v, cand_dout, cand_len, placement
):
    DMA = pltpu.SemaphoreType.DMA

    def half(*shape):
        return pltpu.VMEM(shape, bf16)

    def full(*shape):
        return pltpu.VMEM(shape, f32)

    def result(*shape):
        return jax.ShapeDtypeStruct(shape, bf16)

    oc, dqc, pp, kvp, ck, cv = pl.pallas_call(
        kernel,
        out_shape=(
            result(32, 8192), result(32, 8192), result(16, 8192), result(16, 1024), result(32, 1024), result(32, 1024)
        ),
        in_specs=[SMEM] * 2 + [VMEM] * 4 + [ANY] * 4,
        out_specs=(ANY,) * 6,
        scratch_shapes=[
            half(16, 8192), half(16, 1024), half(8, 16, 128), half(4, 8, 32, 128), half(4, 8, 32, 128),
            half(8, 32, 1024), half(8, 16, 1024), half(8, 32, 1024), half(4, 8, 64, 128), half(4, 8, 64, 128),
            half(LANES, 128), half(LANES, 128), half(2, SPAN, 128), half(2, SPAN, 128),
            half(128, PROMPT), half(128, PROMPT), half(2, 128, SPAN), half(2, 128, SPAN),
            full(KEYS, LANES), half(KEYS, LANES), full(8, LANES), full(8, LANES), full(8, LANES), full(512, 128),
            half(8, 32, 1024), half(8, 32, 1024), half(8, 16, 1024),
            half(3, 8, 64, 128), half(3, 8, 64, 128), half(3, 8, 64, 128), half(3, 8, 64, 128),
            half(8, 64, 128), half(8, 64, 128), half(7, 64, 128), half(7, 64, 128),
            full(8, 64, 128), full(8, 64, 128), full(64, 128),
            half(4, 8, 32, 128), half(4, 8, 32, 128), half(3, 8, 32, 128), half(3, 8, 32, 128),
            half(8, 32, 128), half(8, 32, 128), half(8, 16, 128),
            DMA((12,)), DMA((6, 8)), DMA((6, 8)), DMA((4, 8)), DMA((4, 8)), DMA((4, 4)), DMA((4, 4)),
            DMA((14,)), DMA((14,)), DMA((6, 8)), DMA((6, 8)),
        ],
        compiler_params=pltpu.CompilerParams(
            collective_id=0, has_side_effects=True, vmem_limit_bytes=56 * 2**20
        ),
        name="layer",
    )(
        cand_len, placement,
        prompt_q, prompt_k, prompt_v, prompt_dout, cand_q, cand_k, cand_v, cand_dout,
    )
    return (pp[0:8], pp[8:16], kvp[0:8], kvp[8:16], oc, dqc, ck, cv)


def solution(mesh):
    rows = P(("seq", "head"), None)
    return jax.shard_map(
        local,
        mesh=mesh,
        in_specs=(rows,) * 8 + (P(), P()),
        out_specs=(rows,) * 8,
        check_vma=False,
    )
```

time: 705 us -> 96.9 us (0.14); the launches traced: 692 us -> 96.6 us
  blocking collectives: 331 us -> 0 us
  starting transfers between devices: 132 us -> 0 us
  matrix products: 90.7 us -> 0 us
  Pallas kernels: 0 us -> 89.3 us
  waiting for transfers between devices: 75 us -> 0 us
  local copies, waits for them, and re-layouts: 37.1 us -> 6.67 us
  other arithmetic: 19.4 us -> 0 us
    psum x1 -> x0, blocking collectives: 153 us -> none  [local(): lax.psum((acc_keys[:prompt_all], acc_values[:prompt_all]), 'seq')]
    all_gather x2 -> x0, blocking collectives: 150 us -> none  [the longest x1 76.8 us: local(): lax.all_gather(prompt_value, 'seq', axis=0, tiled=True)]
    all_to_all x14 -> x0, starting transfers between devices: 124 us -> none  [the longest x1 49.1 us: local(): lax.all_to_all(prompt_value_grad.astype(jnp.bfloat16), 'head', split_axis...]
    dot_general x48 -> x0, matrix products: 90.7 us -> none  [the longest x8 18.6 us: head_pass(): jnp.dot(weight_half.T, out_grads, preferred_element_type=jnp.float32)]
    pallas_call x0 -> x1, Pallas kernels: none -> 89.3 us  [local(): pl.pallas_call(kernel, out_shape=(result(32, 8192), result(32, 8192), res...]
    all_to_all x14 -> x0, waiting for transfers between devices: 75 us -> none  [the longest x1 11.9 us: local(): lax.all_to_all(outputs[prompt_dev:], 'head', split_axis=0, concat_axis=1,...]
    all_to_all x2 -> x0, blocking collectives: 28.3 us -> none  [the longest x1 17.2 us: local(): lax.all_to_all(prompt_k, 'head', split_axis=1, concat_axis=0, tiled=True)]
    all_to_all x14 -> x0, local copies, waits for them, and re-layouts: 14.2 us -> none  [the longest x1 1.87 us: local(): lax.all_to_all(cand_q, 'head', split_axis=1, concat_axis=0, tiled=True)]
  transfers between devices with their start and end apart: 18 -> 0, of which waited for: 13 -> 0; matrix products, arithmetic and copies ran while one was open for 4% -> 0% of each run, Pallas kernels for 0% -> 0%
where the time goes in v2:
time: 96.9 us; the launch traced here: 96.6 us
  Pallas kernels  89.3 us (92%)
  local copies, waits for them, and re-layouts  6.67 us (7%)
    pallas_call x1, Pallas kernels, local(): pl.pallas_call(kernel, out_shape=(result(32, 8192), result(32, 8192), res...  89.3 us
    unnamed x12, local copies, waits for them, and re-layouts  3.59 us
    slice x2, local copies, waits for them, and re-layouts, local(): return (pp[0:8], pp[8:16], kvp[0:8], kvp[8:16], oc, dqc, ck, cv)  3.09 us

profile of v2, /device:TPU:1, one launch (start us, length us, event | category | flops | bytes accessed | tf_op | source)
XLA Modules:
  0.0 96.6 jit_solution(6509195945487403371)
XLA Ops:
  0.6 89.3 %layer.1 = (bf16[32,8192]{1,0:T(8,128)(2,1)}, bf16[32,8192]{1,0:T(8,128)(2,1)}, bf16[16,8192]{1,0:T(8,128)(2,1)}, bf16[16,1024]{1,0:T(8,128)(2,1)}, bf16[32,1024]{1,0:T(8,128)(2,1)}, /*index=5*/bf16[32,1024]{1,0:T(8,128)(2,1)}) custom-call(s32[16]{0:T(128)} %cand_len.1, s32[16]{0:T(128)} %placement.1, bf16[8,8192]{1,0:T(8,128)(2,1)} %prompt_q.1, ...), custom_call_target="tpu_custom_call" | custom-call | tf_op jit(solution)/shard_map/layer/pallas_call | solution.py:467
  89.9 0.0 copy-start.1
  89.9 1.7 %fusion = (bf16[8,8192]{1,0:T(8,128)(2,1)}, bf16[8,8192]{1,0:T(8,128)(2,1)}) fusion(bf16[16,8192]{1,0:T(8,128)(2,1)} %get-tuple-element.14), kind=kLoop, calls=%fused_computation | loop fusion | bytes 524288 | tf_op jit(solution)/shard_map/slice | solution.py:497
  91.7 1.3 %fusion.1 = (bf16[8,1024]{1,0:T(8,128)(2,1)}, bf16[8,1024]{1,0:T(8,128)(2,1)}) fusion(bf16[16,1024]{1,0:T(8,128)(2,1)} %get-tuple-element.15), kind=kLoop, calls=%fused_computation.1 | loop fusion | bytes 65536 | tf_op jit(solution)/shard_map/slice | solution.py:497
  93.0 0.0 copy-done.1
  93.0 0.0 copy-start
  93.0 0.8 copy.22
  93.8 0.4 copy-done
  94.3 0.0 copy-start.3
  94.3 0.8 copy.23
  95.1 0.1 copy-done.3
  95.1 0.0 copy-start.2
  95.1 0.6 copy.24
  95.8 0.2 copy-done.2
  96.0 0.6 copy.25
Async XLA Ops:
  89.9 3.1 %copy-start.1 = (bf16[32,8192]{1,0:T(8,128)(2,1)S(1)}, bf16[32,8192]{1,0:T(8,128)(2,1)}, u32[]{:S(2)}) copy-start(bf16[32,8192]{1,0:T(8,128)(2,1)} %get-tuple-element.36) | copy-start | bytes 1572868
  93.0 1.2 %copy-start = (bf16[32,8192]{1,0:T(8,128)(2,1)S(1)}, bf16[32,8192]{1,0:T(8,128)(2,1)}, u32[]{:S(2)}) copy-start(bf16[32,8192]{1,0:T(8,128)(2,1)} %get-tuple-element.37) | copy-start | bytes 1572868
  94.3 0.9 copy-start.3
  95.1 0.9 copy-start.2

commit v3 on v2

--- a/solution.py
+++ b/solution.py
@@ -18,6 +18,7 @@
 PROMPT, SPAN = 2048, 512
 KEYS = PROMPT + SPAN
 LANES = 2560
+WIDE = 512
 
 
 def coords():
@@ -93,7 +94,7 @@
     oc_out, dqc_out, pp_out, kvp_out, ck_out, cv_out,
     pp_stage, kv_stage, kvp_in, kc, vc, qc_in, pp_in, gc_in, kq, vq,
     q_all, g_all, ks, vs, kpt, vpt, kst, vst,
-    scores, halves, peaks, shares, deltas, prompt_out,
+    scores, halves, peaks, shares, deltas, prompt_out, dq,
     oc, dqc, pp, dvb, dkb, rv, rk, zv, zk, zv_in, zk_in, dvown, dkown, vsum,
     dvc, dkc, cv_in, ck_in, cv_sum, ck_sum, psum,
     own, asend, arecv, zsend, zrecv, msend, mrecv, csend, crecv, bsend, brecv,
@@ -137,19 +138,46 @@
     both = kvp_in[...].astype(f32)
     kq[0, z] = both[:, 0:8, :].reshape(64, 128).astype(bf16)
     vq[0, z] = both[:, 8:16, :].reshape(64, 128).astype(bf16)
-    kz = [remote(kq.at[0, z], kq.at[0, z], zsend.at[0, d], zrecv.at[0, d], column[d]) for d in range(1, 8)]
-    vz = [remote(vq.at[0, z], vq.at[0, z], zsend.at[1, d], zrecv.at[1, d], column[d]) for d in range(1, 8)]
-    start(kz)
+    NEAREST = (1, 7, 2, 6, 3, 5, 4)
+
+    def along_z_in(which, kind):
+        moves = {
+            d: remote(which.at[0, z], which.at[0, z], zsend.at[kind, d], zrecv.at[kind, d], column[d]) for d in NEAREST
+        }
+        start(moves.values())
+        return moves
+
+    def forward(which, kind, d):
+        origin = (z + 8 - d) % 8
+        copies = [
+            remote(
+                which.at[0, origin], which.at[p, origin],
+                msend.at[kind, p, d], mrecv.at[kind, p, d], mirror[p],
+            )
+            for p in (1, 2, 3)
+        ]
+        start(copies)
+        return copies
+
+    kz = along_z_in(kq, 0)
+    kquads = [forward(kq, 0, 0)]
     wait(kc_moves)
     kc_near = [
         remote(kc.at[zhi], kc.at[zhi], csend.at[0], crecv.at[0], column[2]),
         remote(kc.at[zhi], kc.at[zhi], csend.at[1], crecv.at[1], column[6]),
     ]
     start(kc_near)
-    start(vz)
-    wait(kz)
-    kquads = [remote(kq.at[0], kq.at[p], msend.at[0, p], mrecv.at[0, p], mirror[p]) for p in (1, 2, 3)]
-    start(kquads)
+    for d in NEAREST:
+        wait([kz[d]])
+        kquads.append(forward(kq, 0, d))
+    vz = along_z_in(vq, 1)
+    vquads = [forward(vq, 1, 0)]
+    wait(vc_moves)
+    vc_near = [
+        remote(vc.at[zhi], vc.at[zhi], csend.at[4], crecv.at[4], column[2]),
+        remote(vc.at[zhi], vc.at[zhi], csend.at[5], crecv.at[5], column[6]),
+    ]
+    start(vc_near)
     below, above = (zhi + 3) % 4, (zhi + 1) % 4
     first, second = pl.ds(0, 4), pl.ds(4, 4)
     wait(kc_near)
@@ -158,15 +186,9 @@
         remote(kc.at[above, second], kc.at[above, second], csend.at[3], crecv.at[3], column[6]),
     ]
     start(kc_far)
-    wait(vc_moves)
-    vc_near = [
-        remote(vc.at[zhi], vc.at[zhi], csend.at[4], crecv.at[4], column[2]),
-        remote(vc.at[zhi], vc.at[zhi], csend.at[5], crecv.at[5], column[6]),
-    ]
-    start(vc_near)
-    wait(vz)
-    vquads = [remote(vq.at[0], vq.at[p], msend.at[1, p], mrecv.at[1, p], mirror[p]) for p in (1, 2, 3)]
-    start(vquads)
+    for d in NEAREST:
+        wait([vz[d]])
+        vquads.append(forward(vq, 1, d))
 
     slots = (1 - sy, sy)
     wait(q_moves)
@@ -184,7 +206,7 @@
         g_all[at : at + 64, :] = both[:, 8:16, :].reshape(64, 128).astype(bf16)
 
     peaks[...] = jnp.full(peaks.shape, HIDDEN, f32)
-    lane = lax.broadcasted_iota(jnp.int32, (1, 256), 1)
+    lane = lax.broadcasted_iota(jnp.int32, (1, WIDE), 1)
     cand_at = ((lane // 64) % 2) * 256 + zhi * 64 + lane % 64
     prompt_at = (
         (z % 2) * 1024 + zhi * 16 + yg * 512 + xg * 128
@@ -192,20 +214,20 @@
     )
 
     def top(s):
-        return jnp.max(s.reshape(-1, 8, 256), axis=0)
+        return jnp.max(s.reshape(-1, 8, WIDE), axis=0)
 
     def score_part(p):
         rows = slice(p * PART, (p + 1) * PART)
         keys = kq[p].reshape(PART, 128)
 
         def cand(t, carry):
-            at = columns(t, 256)
+            at = columns(t, WIDE)
             s = nt(keys, q_all[at, :])
             scores[rows, at] = s
             peaks[:, at] = jnp.maximum(peaks[:, at], top(s))
             return carry
 
-        lax.fori_loop(0, 8, cand, 0)
+        lax.fori_loop(0, 4, cand, 0, unroll=2)
         n = lax.broadcasted_iota(jnp.int32, (PART, 1), 0)
         zz = n // 64
         ygp = yg if p < 2 else 1 - yg
@@ -215,19 +237,14 @@
             + xgp * 128 + ((n // 16) % 2) * 64 + ((n // 8) % 2) * 8 + n % 8
         )
 
-        def prompt(t, carry):
-            at = columns(t, 256)
-            s = jnp.where(key_at <= prompt_at, nt(keys, q_all[at, :]), HIDDEN)
-            scores[rows, at] = s
-            peaks[:, at] = jnp.maximum(peaks[:, at], top(s))
-            return carry
-
-        lax.fori_loop(8, 10, prompt, 0)
+        s = jnp.where(key_at <= prompt_at, nt(keys, q_all[2048:, :]), HIDDEN)
+        scores[rows, 2048:] = s
+        peaks[:, 2048:] = jnp.maximum(peaks[:, 2048:], top(s))
         kpt[:, rows] = keys.astype(f32).T.astype(bf16)
 
     score_part(0)
     for p in (1, 2, 3):
-        wait([kquads[p - 1]])
+        wait([copies[p - 1] for copies in kquads])
         score_part(p)
 
     def slot_rows(source, target, turned):
@@ -250,13 +267,13 @@
     span_at = lax.broadcasted_iota(jnp.int32, (SPAN, 1), 0)
 
     def score_slot(t, carry):
-        at = columns(t, 256)
-        s = jnp.where(span_at <= cand_at, nt(ks[t // 4], q_all[at, :]), HIDDEN)
+        at = columns(t, WIDE)
+        s = jnp.where(span_at <= cand_at, nt(ks[t // 2], q_all[at, :]), HIDDEN)
         scores[PROMPT:, at] = s
         peaks[:, at] = jnp.maximum(peaks[:, at], top(s))
         return carry
 
-    lax.fori_loop(0, 8, score_slot, 0)
+    lax.fori_loop(0, 4, score_slot, 0, unroll=2)
 
     lengths = []
     for i in range(2):
@@ -274,7 +291,8 @@
             for h in range(8):
                 at = i * 1024 + h * 128 + k * 32
                 g_all[at : at + 32, :] = rows[:, h * 128 : (h + 1) * 128]
-    wait(vquads)
+    for copies in vquads:
+        wait(copies)
     for p in range(4):
         vpt[:, p * PART : (p + 1) * PART] = vq[p].reshape(PART, 128).astype(f32).T.astype(bf16)
     wait(vc_far)
@@ -298,7 +316,7 @@
         out = nn(vpt[...], halves[0:PROMPT, at])
         if cand:
             out = out + nn(vst[i], halves[PROMPT:, at])
-            out = jnp.where(cand_at < lengths[i], out, 0.0)
+            out = jnp.where(cand_at[:, 0:256] < lengths[i], out, 0.0)
         delta = jnp.sum(out * g_all[at, :].astype(f32).T, axis=0, keepdims=True)
         deltas[:, at] = jnp.broadcast_to(delta, (8, 256))
         return out.T
@@ -327,14 +345,14 @@
             put_cand(oc, i, pair, weigh(i * 4 + pair, True, i))
             return carry
 
-        lax.fori_loop(0, 4, weigh_cand, 0)
+        lax.fori_loop(0, 4, weigh_cand, 0, unroll=2)
         back += give_back(0, oc, oc_out.at[:, columns(g, 1024)], which)
 
     def weigh_prompt(t, carry):
         prompt_out[columns(t, 256), :] = weigh(8 + t, False, None)
         return carry
 
-    lax.fori_loop(0, 2, weigh_prompt, 0)
+    lax.fori_loop(0, 2, weigh_prompt, 0, unroll=2)
 
     def cand_terms(sums, target, i):
         for half in range(2):
@@ -343,30 +361,31 @@
                     at = half * 256 + hi * 64 + c * 32
                     target[hi, slots[i] * 4 + half * 2 + c] = sums[at : at + 32, :].astype(bf16)
 
-    def terms(others, scale, boxes, mine, inbox, kind, cand_box, cand_inbox):
+    def slot_terms(others, scale, box, inbox, kind):
         for i in range(2):
             rows = slice(i * 1024, (i + 1) * 1024)
-            cand_terms(nn(halves[PROMPT:, rows], others[rows, :]) * scale, cand_box, i)
-        cand_moves = [
+            cand_terms(nn(halves[PROMPT:, rows], others[rows, :]) * scale, box, i)
+        moves = [
             remote(
-                cand_box.at[(zhi + n) % 4], cand_inbox.at[n - 1],
+                box.at[(zhi + n) % 4], inbox.at[n - 1],
                 csend.at[8 + kind * 3 + n - 1], crecv.at[8 + kind * 3 + n - 1], column[2 * n],
             )
             for n in (1, 2, 3)
         ]
-        start(cand_moves)
-        moves = []
-        for p in (3, 1, 2, 0):
-            total = nn(halves[p * PART : (p + 1) * PART, :], others[...]) * scale
-            if p:
-                boxes[p - 1] = total.reshape(8, 64, 128).astype(bf16)
-                moves.append(
-                    remote(boxes.at[p - 1], inbox.at[p - 1], msend.at[2 + kind, p], mrecv.at[2 + kind, p], mirror[p])
-                )
-                start(moves[-1:])
-            else:
-                mine[...] = total.reshape(8, 64, 128)
-        return cand_moves, moves
+        start(moves)
+        return moves
+
+    def terms(others, scale, boxes, mine, inbox, kind, p):
+        total = nn(halves[p * PART : (p + 1) * PART, :], others[...]) * scale
+        if p == 0:
+            mine[...] = total.reshape(8, 64, 128)
+            return []
+        boxes[p - 1] = total.reshape(8, 64, 128).astype(bf16)
+        moves = [
+            remote(boxes.at[p - 1], inbox.at[p - 1], msend.at[2 + kind, p, 0], mrecv.at[2 + kind, p, 0], mirror[p])
+        ]
+        start(moves)
+        return moves
 
     def along_z(mine, inbox, moves, stage, landed, kind):
         wait(moves)
@@ -392,50 +411,63 @@
             box[zhi].astype(f32) + inbox[0].astype(f32) + inbox[1].astype(f32) + inbox[2].astype(f32)
         ).astype(bf16)
 
-    vcand_moves, v_moves = terms(g_all, 1.0, dvb, dvown, rv, 0, dvc, cv_in)
-
-    def grade(t, cand, i):
-        at = columns(t, 256)
-        grads = g_all[at, :]
-        share, delta = shares[0:1, at], deltas[0:1, at]
-        for p in range(PROMPT // PART):
-            rows = slice(p * PART, (p + 1) * PART)
-            dw = nt(vq[p].reshape(PART, 128), grads)
-            halves[rows, at] = (scores[rows, at] * share * (dw - delta)).astype(bf16)
-        dq = nn(kpt[...], halves[0:PROMPT, at])
-        if cand:
-            dw = nt(vs[i], grads)
-            halves[PROMPT:, at] = (scores[PROMPT:, at] * share * (dw - delta)).astype(bf16)
-            dq = dq + nn(kst[i], halves[PROMPT:, at])
-        return (dq * SCALE).T
-
-    def grade_prompt(t, carry):
-        dq = grade(8 + t, False, None)
-        out = prompt_out[columns(t, 256), :]
-        for h in range(4):
-            rows = slice(h * 64, (h + 1) * 64)
-            both = jnp.concatenate([out[rows].reshape(8, 8, 128), dq[rows].reshape(8, 8, 128)], axis=1)
-            pp[:, :, columns(t * 4 + h, 128)] = both.astype(bf16)
+    FARTHEST = (3, 1, 2, 0)
+    vcand_moves = slot_terms(g_all, 1.0, dvc, cv_in, 0)
+    v_moves = []
+    for p in FARTHEST:
+        v_moves += terms(g_all, 1.0, dvb, dvown, rv, 0, p)
+
+    def grade(values, turned, rows, at):
+        dw = nt(values, g_all[at, :])
+        ds = (scores[rows, at] * shares[0:1, at] * (dw - deltas[0:1, at])).astype(bf16)
+        halves[rows, at] = ds
+        return nn(turned, ds)
+
+    def grade_slot(t, carry):
+        at = columns(t, WIDE)
+        dq[:, at] = grade(vs[t // 2], kst[t // 2], slice(PROMPT, KEYS), at)
         return carry
 
-    lax.fori_loop(0, 2, grade_prompt, 0)
-    back += give_back(1, pp, pp_out.at[:, columns(g, 1024)], OTHER + OWN)
-    for i, which in enumerate((OTHER, OWN)):
-
-        def grade_cand(pair, carry, i=i):
-            put_cand(dqc, i, pair, grade(i * 4 + pair, True, i))
+    lax.fori_loop(0, 4, grade_slot, 0, unroll=2)
+    dq[:, 2048:] = jnp.zeros((128, WIDE), f32)
+    kcand_moves = slot_terms(q_all, SCALE, dkc, ck_in, 1)
+
+    def grade_part(p, first, last):
+        rows = slice(p * PART, (p + 1) * PART)
+
+        def body(t, carry):
+            at = columns(t, WIDE)
+            dq[:, at] += grade(vq[p].reshape(PART, 128), kpt[:, rows], rows, at)
             return carry
 
-        lax.fori_loop(0, 4, grade_cand, 0)
-        back += give_back(2, dqc, dqc_out.at[:, columns(g, 1024)], which)
-        if i == 0:
+        lax.fori_loop(first, last, body, 0, unroll=2)
+
+    k_moves = []
+    for n, p in enumerate(FARTHEST[:3]):
+        grade_part(p, 0, 5)
+        k_moves += terms(q_all, SCALE, dkb, dkown, rk, 1, p)
+        if n == 0:
             v_hops = along_z(dvown, rv, v_moves, zv, zv_in, 0)
             cand_final(dvc, cv_in, vcand_moves, cv_sum)
             back += give_back(3, cv_sum, cv_out.at[:, columns(g, 128)], OTHER + OWN)
-
-    kcand_moves, k_moves = terms(q_all, SCALE, dkb, dkown, rk, 1, dkc, ck_in)
+    vsum[...] = final(zv, zv_in, v_hops)
+    for i, which in enumerate((OTHER, OWN)):
+        grade_part(0, i * 2, i * 2 + 2)
+        for pair in range(4):
+            t = i * 4 + pair
+            put_cand(dqc, i, pair, (dq[:, t * 256 : (t + 1) * 256] * SCALE).T)
+        back += give_back(2, dqc, dqc_out.at[:, columns(g, 1024)], which)
+    grade_part(0, 4, 5)
+    terms(q_all, SCALE, dkb, dkown, rk, 1, 0)
     k_hops = along_z(dkown, rk, k_moves, zk, zk_in, 1)
-    vsum[...] = final(zv, zv_in, v_hops)
+    for t in range(2):
+        out = prompt_out[t * 256 : (t + 1) * 256, :]
+        grads = (dq[:, 2048 + t * 256 : 2304 + t * 256] * SCALE).T
+        for h in range(4):
+            rows = slice(h * 64, (h + 1) * 64)
+            both = jnp.concatenate([out[rows].reshape(8, 8, 128), grads[rows].reshape(8, 8, 128)], axis=1)
+            pp[:, :, (t * 4 + h) * 128 : (t * 4 + h + 1) * 128] = both.astype(bf16)
+    back += give_back(1, pp, pp_out.at[:, columns(g, 1024)], OTHER + OWN)
     cand_final(dkc, ck_in, kcand_moves, ck_sum)
     back += give_back(4, ck_sum, ck_out.at[:, columns(g, 128)], OTHER + OWN)
     ksum = final(zk, zk_in, k_hops)
@@ -443,6 +475,19 @@
     psum[...] = both.astype(bf16)
     back += give_back(5, psum, kvp_out.at[:, columns(g, 128)], OTHER + OWN)
     wait(back)
+
+
+def finish_kernel(oc, dqc, pp, kvp, ck, cv, prompt_out, prompt_dq, prompt_dk, prompt_dv, oc_out, dqc_out, ck_out, cv_out, sems):
+    copies = [
+        pltpu.make_async_copy(source, target, sems.at[i])
+        for i, (source, target) in enumerate(((oc, oc_out), (dqc, dqc_out), (ck, ck_out), (cv, cv_out)))
+    ]
+    start(copies)
+    for source, upper, lower in ((pp, prompt_out, prompt_dq), (kvp, prompt_dk, prompt_dv)):
+        both = source[...].astype(f32)
+        upper[...] = both[0:8].astype(bf16)
+        lower[...] = both[8:16].astype(bf16)
+    wait(copies)
 
 
 ANY = pl.BlockSpec(memory_space=pl.ANY)
@@ -476,14 +521,14 @@
             half(8, 32, 1024), half(8, 16, 1024), half(8, 32, 1024), half(4, 8, 64, 128), half(4, 8, 64, 128),
             half(LANES, 128), half(LANES, 128), half(2, SPAN, 128), half(2, SPAN, 128),
             half(128, PROMPT), half(128, PROMPT), half(2, 128, SPAN), half(2, 128, SPAN),
-            full(KEYS, LANES), half(KEYS, LANES), full(8, LANES), full(8, LANES), full(8, LANES), full(512, 128),
+            full(KEYS, LANES), half(KEYS, LANES), full(8, LANES), full(8, LANES), full(8, LANES), full(512, 128), full(128, LANES),
             half(8, 32, 1024), half(8, 32, 1024), half(8, 16, 1024),
             half(3, 8, 64, 128), half(3, 8, 64, 128), half(3, 8, 64, 128), half(3, 8, 64, 128),
             half(8, 64, 128), half(8, 64, 128), half(7, 64, 128), half(7, 64, 128),
             full(8, 64, 128), full(8, 64, 128), full(64, 128),
             half(4, 8, 32, 128), half(4, 8, 32, 128), half(3, 8, 32, 128), half(3, 8, 32, 128),
             half(8, 32, 128), half(8, 32, 128), half(8, 16, 128),
-            DMA((12,)), DMA((6, 8)), DMA((6, 8)), DMA((4, 8)), DMA((4, 8)), DMA((4, 4)), DMA((4, 4)),
+            DMA((12,)), DMA((6, 8)), DMA((6, 8)), DMA((4, 8)), DMA((4, 8)), DMA((4, 4, 8)), DMA((4, 4, 8)),
             DMA((14,)), DMA((14,)), DMA((6, 8)), DMA((6, 8)),
         ],
         compiler_params=pltpu.CompilerParams(
@@ -494,7 +539,17 @@
         cand_len, placement,
         prompt_q, prompt_k, prompt_v, prompt_dout, cand_q, cand_k, cand_v, cand_dout,
     )
-    return (pp[0:8], pp[8:16], kvp[0:8], kvp[8:16], oc, dqc, ck, cv)
+    return pl.pallas_call(
+        finish_kernel,
+        out_shape=(
+            result(8, 8192), result(8, 8192), result(8, 1024), result(8, 1024),
+            result(32, 8192), result(32, 8192), result(32, 1024), result(32, 1024),
+        ),
+        in_specs=[ANY, ANY, VMEM, VMEM, ANY, ANY],
+        out_specs=(VMEM,) * 4 + (ANY,) * 4,
+        scratch_shapes=[DMA((4,))],
+        name="finish",
+    )(oc, dqc, pp, kvp, ck, cv)
 
 
 def solution(mesh):

time: 96.9 us -> 123 us (1.27)
  Pallas kernels: 89.3 us -> 123 us
  local copies, waits for them, and re-layouts: 6.67 us -> 0 us
    pallas_call x0 -> x1, Pallas kernels: none -> 38.5 us  [local(): pl.pallas_call(finish_kernel, out_shape=(result(8, 8192), result(8, 8192)...]
    pallas_call x1, Pallas kernels: 89.3 us -> 84 us  [local(): pl.pallas_call(kernel, out_shape=(result(32, 8192), result(32, 8192), res...]
    unnamed x12 -> x0, local copies, waits for them, and re-layouts: 3.59 us -> none
    slice x2 -> x0, local copies, waits for them, and re-layouts: 3.09 us -> none  [local(): return (pp[0:8], pp[8:16], kvp[0:8], kvp[8:16], oc, dqc, ck, cv)]
where the time goes in v3:
time: 123 us
  Pallas kernels  123 us (100%)
    pallas_call x1, Pallas kernels, local(): pl.pallas_call(kernel, out_shape=(result(32, 8192), result(32, 8192), res...  84 us
    pallas_call x1, Pallas kernels, local(): pl.pallas_call(finish_kernel, out_shape=(result(8, 8192), result(8, 8192)...  38.5 us

profile of v3, /device:TPU:1, one launch (start us, length us, event | category | flops | bytes accessed | tf_op | source)
XLA Modules:
  0.0 123.4 jit_solution(6974435617889483513)
XLA Ops:
  0.6 84.0 %layer.1 = (bf16[32,8192]{1,0:T(8,128)(2,1)}, bf16[32,8192]{1,0:T(8,128)(2,1)}, bf16[16,8192]{1,0:T(8,128)(2,1)}, bf16[16,1024]{1,0:T(8,128)(2,1)}, bf16[32,1024]{1,0:T(8,128)(2,1)}, /*index=5*/bf16[32,1024]{1,0:T(8,128)(2,1)}) custom-call(s32[16]{0:T(128)} %cand_len.1, s32[16]{0:T(128)} %placement.1, bf16[8,8192]{1,0:T(8,128)(2,1)} %prompt_q.1, ...), custom_call_target="tpu_custom_call" | custom-call | tf_op jit(solution)/shard_map/layer/pallas_call | solution.py:512
  84.7 38.5 %finish.1 = (bf16[8,8192]{1,0:T(8,128)(2,1)}, bf16[8,8192]{1,0:T(8,128)(2,1)}, bf16[8,1024]{1,0:T(8,128)(2,1)}, bf16[8,1024]{1,0:T(8,128)(2,1)}, bf16[32,8192]{1...) custom-call(bf16[32,8192]{1,0:T(8,128)(2,1)} %get-tuple-element.14.oc, ...), custom_call_target="tpu_custom_call" | custom-call | tf_op jit(solution)/shard_map/finish/pallas_call | solution.py:542

commit v4 on v3

--- a/solution.py
+++ b/solution.py
@@ -71,9 +71,8 @@
         copy.start()
 
 
-def wait(copies):
-    for copy in copies:
-        copy.wait()
+def take(sem, ref):
+    pltpu.make_async_copy(ref, ref, sem).wait()
 
 
 def nt(a, b):
@@ -89,7 +88,7 @@
 
 
 def kernel(
-    cand_len, placement,
+    cand_len_in, placement_in,
     prompt_q, prompt_k, prompt_v, prompt_dout, cand_q, cand_k, cand_v, cand_dout,
     oc_out, dqc_out, pp_out, kvp_out, ck_out, cv_out,
     pp_stage, kv_stage, kvp_in, kc, vc, qc_in, pp_in, gc_in, kq, vq,
@@ -97,7 +96,7 @@
     scores, halves, peaks, shares, deltas, prompt_out, dq,
     oc, dqc, pp, dvb, dkb, rv, rk, zv, zk, zv_in, zk_in, dvown, dkown, vsum,
     dvc, dkc, cv_in, ck_in, cv_sum, ck_sum, psum,
-    own, asend, arecv, zsend, zrecv, msend, mrecv, csend, crecv, bsend, brecv,
+    cand_len, placement, lsem, asend, arecv, zsend, zrecv, msend, mrecv, csend, crecv, bsend, brecv,
 ):
     x, y, z, core = coords()
     xg, yg, j, g = roles(x, y, core)
@@ -108,6 +107,11 @@
     }
     column = {d: device(x, y, (z + d) % 8, core) for d in range(1, 8)}
 
+    small = [
+        pltpu.make_async_copy(cand_len_in, cand_len, lsem.at[0]),
+        pltpu.make_async_copy(placement_in, placement, lsem.at[1]),
+    ]
+    start(small)
     both = jnp.concatenate([prompt_k[...].astype(f32), prompt_v[...].astype(f32)], axis=0)
     kv_stage[...] = both.astype(bf16)
     both = jnp.concatenate([prompt_q[...].astype(f32), prompt_dout[...].astype(f32)], axis=0)
@@ -115,90 +119,88 @@
 
     greet(list(block.values()) + list(mirror.values()) + list(column.values()))
 
+    late = []
+
     def exchange(kind, source, width, target):
-        copies = [pltpu.make_async_copy(source.at[:, columns(g, width)], target, own.at[kind])]
-        for d in range(1, 8):
-            copies.append(
-                remote(
-                    source.at[:, columns(flip(g, d), width)], target,
-                    asend.at[kind, d], arecv.at[kind, d], block[d],
-                )
-            )
-        start(copies)
-        return copies
-
-    kvp_moves = exchange(0, kv_stage, 128, kvp_in.at[j])
-    kc_moves = exchange(1, cand_k, 128, kc.at[zhi, j])
-    q_moves = exchange(2, cand_q, 1024, qc_in.at[j])
-    pp_moves = exchange(3, pp_stage, 1024, pp_in.at[j])
-    vc_moves = exchange(4, cand_v, 128, vc.at[zhi, j])
-    g_moves = exchange(5, cand_dout, 1024, gc_in.at[j])
-
-    wait(kvp_moves)
+        start([pltpu.make_async_copy(source.at[:, columns(g, width)], target.at[j], arecv.at[kind])])
+        start(
+            [
+                remote(source.at[:, columns(flip(g, d), width)], target.at[j], asend.at[kind], arecv.at[kind], block[d])
+                for d in range(1, 8)
+            ]
+        )
+        late.append((asend.at[kind], target.at[pl.ds(0, 7)]))
+
+    exchange(0, kv_stage, 128, kvp_in)
+    exchange(1, cand_k, 128, kc.at[zhi])
+    exchange(2, cand_q, 1024, qc_in)
+    exchange(3, pp_stage, 1024, pp_in)
+    exchange(4, cand_v, 128, vc.at[zhi])
+    exchange(5, cand_dout, 1024, gc_in)
+
+    below, above = (zhi + 3) % 4, (zhi + 1) % 4
+    first, second = pl.ds(0, 4), pl.ds(4, 4)
+
+    def along_z_in(which, kind):
+        start(
+            [
+                remote(which.at[0, z], which.at[0, z], zsend.at[kind], zrecv.at[kind], column[d])
+                for d in (1, 7, 2, 6, 3, 5, 4)
+            ]
+        )
+        late.append((zsend.at[kind], which.at[0, pl.ds(0, 7)]))
+
+    def quadrants(which, kind):
+        take(zrecv.at[kind], which.at[0, pl.ds(0, 7)])
+        start(
+            [
+                remote(which.at[0], which.at[p], msend.at[kind], mrecv.at[kind, p], mirror[p])
+                for p in (1, 2, 3)
+            ]
+        )
+        late.append((msend.at[kind], which.at[pl.ds(0, 3)]))
+
+    def near(which, kind):
+        take(arecv.at[1 + 3 * kind], which.at[zhi])
+        start(
+            [
+                remote(which.at[zhi], which.at[zhi], csend.at[kind], crecv.at[kind], column[d])
+                for d in (2, 6)
+            ]
+        )
+        late.append((csend.at[kind], which.at[pl.ds(0, 2)]))
+
+    def far(which, kind):
+        take(crecv.at[kind], which.at[pl.ds(0, 2)])
+        start(
+            [
+                remote(which.at[below, first], which.at[below, first], csend.at[2 + kind], crecv.at[2 + kind], column[2]),
+                remote(which.at[above, second], which.at[above, second], csend.at[2 + kind], crecv.at[2 + kind], column[6]),
+            ]
+        )
+        late.append((csend.at[2 + kind], which.at[0]))
+
+    take(arecv.at[0], kvp_in)
     both = kvp_in[...].astype(f32)
     kq[0, z] = both[:, 0:8, :].reshape(64, 128).astype(bf16)
     vq[0, z] = both[:, 8:16, :].reshape(64, 128).astype(bf16)
-    NEAREST = (1, 7, 2, 6, 3, 5, 4)
-
-    def along_z_in(which, kind):
-        moves = {
-            d: remote(which.at[0, z], which.at[0, z], zsend.at[kind, d], zrecv.at[kind, d], column[d]) for d in NEAREST
-        }
-        start(moves.values())
-        return moves
-
-    def forward(which, kind, d):
-        origin = (z + 8 - d) % 8
-        copies = [
-            remote(
-                which.at[0, origin], which.at[p, origin],
-                msend.at[kind, p, d], mrecv.at[kind, p, d], mirror[p],
-            )
-            for p in (1, 2, 3)
-        ]
-        start(copies)
-        return copies
-
-    kz = along_z_in(kq, 0)
-    kquads = [forward(kq, 0, 0)]
-    wait(kc_moves)
-    kc_near = [
-        remote(kc.at[zhi], kc.at[zhi], csend.at[0], crecv.at[0], column[2]),
-        remote(kc.at[zhi], kc.at[zhi], csend.at[1], crecv.at[1], column[6]),
-    ]
-    start(kc_near)
-    for d in NEAREST:
-        wait([kz[d]])
-        kquads.append(forward(kq, 0, d))
-    vz = along_z_in(vq, 1)
-    vquads = [forward(vq, 1, 0)]
-    wait(vc_moves)
-    vc_near = [
-        remote(vc.at[zhi], vc.at[zhi], csend.at[4], crecv.at[4], column[2]),
-        remote(vc.at[zhi], vc.at[zhi], csend.at[5], crecv.at[5], column[6]),
-    ]
-    start(vc_near)
-    below, above = (zhi + 3) % 4, (zhi + 1) % 4
-    first, second = pl.ds(0, 4), pl.ds(4, 4)
-    wait(kc_near)
-    kc_far = [
-        remote(kc.at[below, first], kc.at[below, first], csend.at[2], crecv.at[2], column[2]),
-        remote(kc.at[above, second], kc.at[above, second], csend.at[3], crecv.at[3], column[6]),
-    ]
-    start(kc_far)
-    for d in NEAREST:
-        wait([vz[d]])
-        vquads.append(forward(vq, 1, d))
+    along_z_in(kq, 0)
+    near(kc, 0)
+    along_z_in(vq, 1)
+    quadrants(kq, 0)
+    far(kc, 0)
+    near(vc, 1)
+    quadrants(vq, 1)
 
     slots = (1 - sy, sy)
-    wait(q_moves)
+    take(arecv.at[2], qc_in)
     for i in range(2):
         for k in range(4):
             rows = qc_in[slots[i] * 4 + k]
             for h in range(8):
                 at = i * 1024 + h * 128 + k * 32
                 q_all[at : at + 32, :] = rows[:, h * 128 : (h + 1) * 128]
-    wait(pp_moves)
+    take(arecv.at[3], pp_in)
     for h in range(8):
         both = pp_in[:, :, h * 128 : (h + 1) * 128].astype(f32)
         at = 2048 + h * 64
@@ -244,7 +246,7 @@
 
     score_part(0)
     for p in (1, 2, 3):
-        wait([copies[p - 1] for copies in kquads])
+        take(mrecv.at[0, p], kq.at[p])
         score_part(p)
 
     def slot_rows(source, target, turned):
@@ -256,13 +258,8 @@
                         target[i, at : at + 32, :] = source[hi, slots[i] * 4 + half * 2 + c]
             turned[i] = target[i].astype(f32).T.astype(bf16)
 
-    wait(vc_near)
-    vc_far = [
-        remote(vc.at[below, first], vc.at[below, first], csend.at[6], crecv.at[6], column[2]),
-        remote(vc.at[above, second], vc.at[above, second], csend.at[7], crecv.at[7], column[6]),
-    ]
-    start(vc_far)
-    wait(kc_far)
+    far(vc, 1)
+    take(crecv.at[2], kc.at[0])
     slot_rows(kc, ks, kst)
     span_at = lax.broadcasted_iota(jnp.int32, (SPAN, 1), 0)
 
@@ -275,6 +272,8 @@
 
     lax.fori_loop(0, 4, score_slot, 0, unroll=2)
 
+    small[0].wait()
+    small[1].wait()
     lengths = []
     for i in range(2):
         slot = (z % 2) * 8 + ((y // 2) * 2 + slots[i]) * 2 + x // 2
@@ -282,7 +281,7 @@
         for c in range(16):
             length = length + jnp.where(placement[c] == slot, cand_len[c], 0)
         lengths.append(length)
-    wait(g_moves)
+    take(arecv.at[5], gc_in)
     row = lax.broadcasted_iota(jnp.int32, (32, 1), 0)
     for i in range(2):
         for k in range(4):
@@ -291,11 +290,11 @@
             for h in range(8):
                 at = i * 1024 + h * 128 + k * 32
                 g_all[at : at + 32, :] = rows[:, h * 128 : (h + 1) * 128]
-    for copies in vquads:
-        wait(copies)
+    for p in (1, 2, 3):
+        take(mrecv.at[1, p], vq.at[p])
     for p in range(4):
         vpt[:, p * PART : (p + 1) * PART] = vq[p].reshape(PART, 128).astype(f32).T.astype(bf16)
-    wait(vc_far)
+    take(crecv.at[3], vc.at[0])
     slot_rows(vc, vs, vst)
 
     def weigh(t, cand, i):
@@ -327,18 +326,15 @@
                 at = a * 128 + k * 32
                 target[slots[i] * 4 + k, :, columns(pair * 2 + a, 128)] = rows[at : at + 32, :].astype(bf16)
 
-    def give_back(kind, source, target, which):
-        copies = []
+    def give_back(kind, source, target, width, which):
+        here = target.at[:, columns(g, width)]
         if 0 in which:
-            copies.append(pltpu.make_async_copy(source.at[j], target, own.at[6 + kind]))
-        for d in which:
-            if d:
-                copies.append(remote(source.at[flip(j, d)], target, bsend.at[kind, d], brecv.at[kind, d], block[d]))
-        start(copies)
-        return copies
+            start([pltpu.make_async_copy(source.at[j], here, brecv.at[kind])])
+            late.append((bsend.at[kind], source.at[pl.ds(0, 7)]))
+            late.append((brecv.at[kind], target))
+        start([remote(source.at[flip(j, d)], here, bsend.at[kind], brecv.at[kind], block[d]) for d in which if d])
 
     OTHER, OWN = (4, 5, 6, 7), (1, 2, 3, 0)
-    back = []
     for i, which in enumerate((OTHER, OWN)):
 
         def weigh_cand(pair, carry, i=i):
@@ -346,7 +342,7 @@
             return carry
 
         lax.fori_loop(0, 4, weigh_cand, 0, unroll=2)
-        back += give_back(0, oc, oc_out.at[:, columns(g, 1024)], which)
+        give_back(0, oc, oc_out, 1024, which)
 
     def weigh_prompt(t, carry):
         prompt_out[columns(t, 256), :] = weigh(8 + t, False, None)
@@ -365,57 +361,52 @@
         for i in range(2):
             rows = slice(i * 1024, (i + 1) * 1024)
             cand_terms(nn(halves[PROMPT:, rows], others[rows, :]) * scale, box, i)
-        moves = [
-            remote(
-                box.at[(zhi + n) % 4], inbox.at[n - 1],
-                csend.at[8 + kind * 3 + n - 1], crecv.at[8 + kind * 3 + n - 1], column[2 * n],
-            )
-            for n in (1, 2, 3)
-        ]
-        start(moves)
-        return moves
+        start(
+            [
+                remote(box.at[(zhi + n) % 4], inbox.at[n - 1], csend.at[4 + kind], crecv.at[4 + kind], column[2 * n])
+                for n in (1, 2, 3)
+            ]
+        )
+        late.append((csend.at[4 + kind], inbox))
 
     def terms(others, scale, boxes, mine, inbox, kind, p):
         total = nn(halves[p * PART : (p + 1) * PART, :], others[...]) * scale
         if p == 0:
             mine[...] = total.reshape(8, 64, 128)
-            return []
+            late.append((msend.at[2 + kind], inbox))
+            return
         boxes[p - 1] = total.reshape(8, 64, 128).astype(bf16)
-        moves = [
-            remote(boxes.at[p - 1], inbox.at[p - 1], msend.at[2 + kind, p, 0], mrecv.at[2 + kind, p, 0], mirror[p])
-        ]
-        start(moves)
-        return moves
-
-    def along_z(mine, inbox, moves, stage, landed, kind):
-        wait(moves)
+        start([remote(boxes.at[p - 1], inbox.at[p - 1], msend.at[2 + kind], mrecv.at[2 + kind, 0], mirror[p])])
+
+    def along_z(mine, inbox, stage, landed, kind):
+        take(mrecv.at[2 + kind, 0], inbox)
         total = mine[...] + inbox[0].astype(f32) + inbox[1].astype(f32) + inbox[2].astype(f32)
         stage[...] = total.astype(bf16)
-        hops = [
-            remote(stage.at[(z + d) % 8], landed.at[d - 1], zsend.at[2 + kind, d], zrecv.at[2 + kind, d], column[d])
-            for d in range(1, 8)
-        ]
-        start(hops)
-        return hops
-
-    def final(stage, landed, hops):
-        wait(hops)
+        start(
+            [
+                remote(stage.at[(z + d) % 8], landed.at[d - 1], zsend.at[2 + kind], zrecv.at[2 + kind], column[d])
+                for d in (4, 3, 5, 2, 6, 1, 7)
+            ]
+        )
+        late.append((zsend.at[2 + kind], landed))
+
+    def final(stage, landed, kind):
+        take(zrecv.at[2 + kind], landed)
         total = stage[z].astype(f32)
         for d in range(7):
             total = total + landed[d].astype(f32)
         return total
 
-    def cand_final(box, inbox, moves, total):
-        wait(moves)
+    def cand_final(box, inbox, total, kind):
+        take(crecv.at[4 + kind], inbox)
         total[...] = (
             box[zhi].astype(f32) + inbox[0].astype(f32) + inbox[1].astype(f32) + inbox[2].astype(f32)
         ).astype(bf16)
 
     FARTHEST = (3, 1, 2, 0)
-    vcand_moves = slot_terms(g_all, 1.0, dvc, cv_in, 0)
-    v_moves = []
+    slot_terms(g_all, 1.0, dvc, cv_in, 0)
     for p in FARTHEST:
-        v_moves += terms(g_all, 1.0, dvb, dvown, rv, 0, p)
+        terms(g_all, 1.0, dvb, dvown, rv, 0, p)
 
     def grade(values, turned, rows, at):
         dw = nt(values, g_all[at, :])
@@ -430,7 +421,7 @@
 
     lax.fori_loop(0, 4, grade_slot, 0, unroll=2)
     dq[:, 2048:] = jnp.zeros((128, WIDE), f32)
-    kcand_moves = slot_terms(q_all, SCALE, dkc, ck_in, 1)
+    slot_terms(q_all, SCALE, dkc, ck_in, 1)
 
     def grade_part(p, first, last):
         rows = slice(p * PART, (p + 1) * PART)
@@ -442,24 +433,23 @@
 
         lax.fori_loop(first, last, body, 0, unroll=2)
 
-    k_moves = []
     for n, p in enumerate(FARTHEST[:3]):
         grade_part(p, 0, 5)
-        k_moves += terms(q_all, SCALE, dkb, dkown, rk, 1, p)
+        terms(q_all, SCALE, dkb, dkown, rk, 1, p)
         if n == 0:
-            v_hops = along_z(dvown, rv, v_moves, zv, zv_in, 0)
-            cand_final(dvc, cv_in, vcand_moves, cv_sum)
-            back += give_back(3, cv_sum, cv_out.at[:, columns(g, 128)], OTHER + OWN)
-    vsum[...] = final(zv, zv_in, v_hops)
+            along_z(dvown, rv, zv, zv_in, 0)
+            cand_final(dvc, cv_in, cv_sum, 0)
+            give_back(3, cv_sum, cv_out, 128, OTHER + OWN)
+    vsum[...] = final(zv, zv_in, 0)
     for i, which in enumerate((OTHER, OWN)):
         grade_part(0, i * 2, i * 2 + 2)
         for pair in range(4):
             t = i * 4 + pair
             put_cand(dqc, i, pair, (dq[:, t * 256 : (t + 1) * 256] * SCALE).T)
-        back += give_back(2, dqc, dqc_out.at[:, columns(g, 1024)], which)
+        give_back(2, dqc, dqc_out, 1024, which)
     grade_part(0, 4, 5)
     terms(q_all, SCALE, dkb, dkown, rk, 1, 0)
-    k_hops = along_z(dkown, rk, k_moves, zk, zk_in, 1)
+    along_z(dkown, rk, zk, zk_in, 1)
     for t in range(2):
         out = prompt_out[t * 256 : (t + 1) * 256, :]
         grads = (dq[:, 2048 + t * 256 : 2304 + t * 256] * SCALE).T
@@ -467,14 +457,15 @@
             rows = slice(h * 64, (h + 1) * 64)
             both = jnp.concatenate([out[rows].reshape(8, 8, 128), grads[rows].reshape(8, 8, 128)], axis=1)
             pp[:, :, (t * 4 + h) * 128 : (t * 4 + h + 1) * 128] = both.astype(bf16)
-    back += give_back(1, pp, pp_out.at[:, columns(g, 1024)], OTHER + OWN)
-    cand_final(dkc, ck_in, kcand_moves, ck_sum)
-    back += give_back(4, ck_sum, ck_out.at[:, columns(g, 128)], OTHER + OWN)
-    ksum = final(zk, zk_in, k_hops)
+    give_back(1, pp, pp_out, 1024, OTHER + OWN)
+    cand_final(dkc, ck_in, ck_sum, 1)
+    give_back(4, ck_sum, ck_out, 128, OTHER + OWN)
+    ksum = final(zk, zk_in, 1)
     both = jnp.concatenate([ksum.reshape(8, 8, 128), vsum[...].reshape(8, 8, 128)], axis=1)
     psum[...] = both.astype(bf16)
-    back += give_back(5, psum, kvp_out.at[:, columns(g, 128)], OTHER + OWN)
-    wait(back)
+    give_back(5, psum, kvp_out, 128, OTHER + OWN)
+    for sem, ref in late:
+        take(sem, ref)
 
 
 def finish_kernel(oc, dqc, pp, kvp, ck, cv, prompt_out, prompt_dq, prompt_dk, prompt_dv, oc_out, dqc_out, ck_out, cv_out, sems):
@@ -487,12 +478,12 @@
         both = source[...].astype(f32)
         upper[...] = both[0:8].astype(bf16)
         lower[...] = both[8:16].astype(bf16)
-    wait(copies)
+    for copy in copies:
+        copy.wait()
 
 
 ANY = pl.BlockSpec(memory_space=pl.ANY)
 VMEM = pl.BlockSpec(memory_space=pltpu.VMEM)
-SMEM = pl.BlockSpec(memory_space=pltpu.SMEM)
 
 
 def local(
@@ -514,7 +505,7 @@
         out_shape=(
             result(32, 8192), result(32, 8192), result(16, 8192), result(16, 1024), result(32, 1024), result(32, 1024)
         ),
-        in_specs=[SMEM] * 2 + [VMEM] * 4 + [ANY] * 4,
+        in_specs=[ANY] * 2 + [VMEM] * 4 + [ANY] * 4,
         out_specs=(ANY,) * 6,
         scratch_shapes=[
             half(16, 8192), half(16, 1024), half(8, 16, 128), half(4, 8, 32, 128), half(4, 8, 32, 128),
@@ -528,8 +519,9 @@
             full(8, 64, 128), full(8, 64, 128), full(64, 128),
             half(4, 8, 32, 128), half(4, 8, 32, 128), half(3, 8, 32, 128), half(3, 8, 32, 128),
             half(8, 32, 128), half(8, 32, 128), half(8, 16, 128),
-            DMA((12,)), DMA((6, 8)), DMA((6, 8)), DMA((4, 8)), DMA((4, 8)), DMA((4, 4, 8)), DMA((4, 4, 8)),
-            DMA((14,)), DMA((14,)), DMA((6, 8)), DMA((6, 8)),
+            pltpu.SMEM((16,), jnp.int32), pltpu.SMEM((16,), jnp.int32),
+            DMA((2,)), DMA((6,)), DMA((6,)), DMA((4,)), DMA((4,)), DMA((4,)), DMA((4, 4)),
+            DMA((6,)), DMA((6,)), DMA((6,)), DMA((6,)),
         ],
         compiler_params=pltpu.CompilerParams(
             collective_id=0, has_side_effects=True, vmem_limit_bytes=56 * 2**20
@@ -545,7 +537,7 @@
             result(8, 8192), result(8, 8192), result(8, 1024), result(8, 1024),
             result(32, 8192), result(32, 8192), result(32, 1024), result(32, 1024),
         ),
-        in_specs=[ANY, ANY, VMEM, VMEM, ANY, ANY],
+        in_specs=[VMEM] * 6,
         out_specs=(VMEM,) * 4 + (ANY,) * 4,
         scratch_shapes=[DMA((4,))],
         name="finish",

time: 123 us -> 80.7 us (0.66)
  Pallas kernels: 123 us -> 79.8 us
    pallas_call x1, Pallas kernels: 38.5 us -> 3.03 us  [local(): pl.pallas_call(finish_kernel, out_shape=(result(8, 8192), result(8, 8192)...]
    pallas_call x1, Pallas kernels: 84 us -> 76.7 us  [local(): pl.pallas_call(kernel, out_shape=(result(32, 8192), result(32, 8192), res...]
where the time goes in v4:
time: 80.7 us; the launch traced here: 80.6 us
  Pallas kernels  79.8 us (99%)
  between operations  0.81 us (1%)
    pallas_call x1, Pallas kernels, local(): pl.pallas_call(kernel, out_shape=(result(32, 8192), result(32, 8192), res...  76.7 us
    pallas_call x1, Pallas kernels, local(): pl.pallas_call(finish_kernel, out_shape=(result(8, 8192), result(8, 8192)...  3.03 us

profile of v4, /device:TPU:1, one launch (start us, length us, event | category | flops | bytes accessed | tf_op | source)
XLA Modules:
  0.0 80.6 jit_solution(12479974549684390010)
XLA Ops:
  0.6 76.7 %layer.1 = (bf16[32,8192]{1,0:T(8,128)(2,1)}, bf16[32,8192]{1,0:T(8,128)(2,1)}, bf16[16,8192]{1,0:T(8,128)(2,1)}, bf16[16,1024]{1,0:T(8,128)(2,1)}, bf16[32,1024]{1,0:T(8,128)(2,1)}, /*index=5*/bf16[32,1024]{1,0:T(8,128)(2,1)}) custom-call(s32[16]{0:T(128)} %cand_len_in.1, s32[16]{0:T(128)} %placement_in.1, bf16[8,8192]{1,0:T(8,128)(2,1)} %prompt_q.1, ...), custom_call_target="tpu_custom_call" | custom-call | tf_op jit(solution)/shard_map/layer/pallas_call | solution.py:503
  77.4 3.0 %finish.1 = (bf16[8,8192]{1,0:T(8,128)(2,1)}, bf16[8,8192]{1,0:T(8,128)(2,1)}, bf16[8,1024]{1,0:T(8,128)(2,1)}, bf16[8,1024]{1,0:T(8,128)(2,1)}, bf16[32,8192]{1...) custom-call(bf16[32,8192]{1,0:T(8,128)(2,1)} %get-tuple-element.14.oc, ...), custom_call_target="tpu_custom_call" | custom-call | tf_op jit(solution)/shard_map/finish/pallas_call | solution.py:534

commit v5 on v4

--- a/solution.py
+++ b/solution.py
@@ -84,6 +84,8 @@
 
 
 def columns(index, width):
+    if isinstance(index, int):
+        return pl.ds(index * width, width)
     return pl.ds(pl.multiple_of(index * width, width), width)
 
 
@@ -93,8 +95,8 @@
     oc_out, dqc_out, pp_out, kvp_out, ck_out, cv_out,
     pp_stage, kv_stage, kvp_in, kc, vc, qc_in, pp_in, gc_in, kq, vq,
     q_all, g_all, ks, vs, kpt, vpt, kst, vst,
-    scores, halves, peaks, shares, deltas, prompt_out, dq,
-    oc, dqc, pp, dvb, dkb, rv, rk, zv, zk, zv_in, zk_in, dvown, dkown, vsum,
+    scores, halves, slot_scores, slot_halves, peaks, shares, deltas, prompt_out, dq,
+    dvb, dkb, rv, rk, zv, zk, zv_in, zk_in, dvown, dkown, vsum,
     dvc, dkc, cv_in, ck_in, cv_sum, ck_sum, psum,
     cand_len, placement, lsem, asend, arecv, zsend, zrecv, msend, mrecv, csend, crecv, bsend, brecv,
 ):
@@ -138,26 +140,33 @@
     exchange(4, cand_v, 128, vc.at[zhi])
     exchange(5, cand_dout, 1024, gc_in)
 
+    CLOSE, DISTANT = (1, 7, 2, 6), (3, 5, 4)
     below, above = (zhi + 3) % 4, (zhi + 1) % 4
     first, second = pl.ds(0, 4), pl.ds(4, 4)
 
     def along_z_in(which, kind):
         start(
             [
-                remote(which.at[0, z], which.at[0, z], zsend.at[kind], zrecv.at[kind], column[d])
-                for d in (1, 7, 2, 6, 3, 5, 4)
+                remote(
+                    which.at[0, z], which.at[0, z], zsend.at[kind],
+                    zrecv.at[kind if d in CLOSE else 4 + kind], column[d],
+                )
+                for d in CLOSE + DISTANT
             ]
         )
         late.append((zsend.at[kind], which.at[0, pl.ds(0, 7)]))
 
+    def forward(which, kind, steps):
+        for d in steps:
+            at = (z + 8 - d) % 8
+            start([remote(which.at[0, at], which.at[p, at], msend.at[kind], mrecv.at[kind, p], mirror[p]) for p in (1, 2, 3)])
+
     def quadrants(which, kind):
-        take(zrecv.at[kind], which.at[0, pl.ds(0, 7)])
-        start(
-            [
-                remote(which.at[0], which.at[p], msend.at[kind], mrecv.at[kind, p], mirror[p])
-                for p in (1, 2, 3)
-            ]
-        )
+        forward(which, kind, (0,))
+        take(zrecv.at[kind], which.at[0, pl.ds(0, 4)])
+        forward(which, kind, CLOSE)
+        take(zrecv.at[4 + kind], which.at[0, pl.ds(0, 3)])
+        forward(which, kind, DISTANT)
         late.append((msend.at[kind], which.at[pl.ds(0, 3)]))
 
     def near(which, kind):
@@ -207,7 +216,6 @@
         q_all[at : at + 64, :] = both[:, 0:8, :].reshape(64, 128).astype(bf16)
         g_all[at : at + 64, :] = both[:, 8:16, :].reshape(64, 128).astype(bf16)
 
-    peaks[...] = jnp.full(peaks.shape, HIDDEN, f32)
     lane = lax.broadcasted_iota(jnp.int32, (1, WIDE), 1)
     cand_at = ((lane // 64) % 2) * 256 + zhi * 64 + lane % 64
     prompt_at = (
@@ -215,8 +223,18 @@
         + ((lane // 32) % 2) * 256 + ((lane // 16) % 2) * 64 + ((lane // 8) % 2) * 8 + lane % 8
     )
 
-    def top(s):
-        return jnp.max(s.reshape(-1, 8, WIDE), axis=0)
+    def part_scores(p):
+        return slot_scores if p == 4 else scores.at[p * PART : (p + 1) * PART]
+
+    def part_halves(p):
+        return slot_halves if p == 4 else halves.at[p * PART : (p + 1) * PART]
+
+    def weigh_part(p, at, s):
+        peak = jnp.max(jnp.max(s.reshape(-1, 8, WIDE), axis=0), axis=0, keepdims=True)
+        e = jnp.exp2((s - peak) * SCALE2)
+        part_scores(p)[:, at] = e
+        peaks[p, :, at] = jnp.broadcast_to(peak, (8, WIDE))
+        shares[p, :, at] = jnp.sum(e.reshape(-1, 8, WIDE), axis=0)
 
     def score_part(p):
         rows = slice(p * PART, (p + 1) * PART)
@@ -224,12 +242,10 @@
 
         def cand(t, carry):
             at = columns(t, WIDE)
-            s = nt(keys, q_all[at, :])
-            scores[rows, at] = s
-            peaks[:, at] = jnp.maximum(peaks[:, at], top(s))
+            weigh_part(p, at, nt(keys, q_all[at, :]))
             return carry
 
-        lax.fori_loop(0, 4, cand, 0, unroll=2)
+        lax.fori_loop(0, 4, cand, 0, unroll=4)
         n = lax.broadcasted_iota(jnp.int32, (PART, 1), 0)
         zz = n // 64
         ygp = yg if p < 2 else 1 - yg
@@ -239,9 +255,7 @@
             + xgp * 128 + ((n // 16) % 2) * 64 + ((n // 8) % 2) * 8 + n % 8
         )
 
-        s = jnp.where(key_at <= prompt_at, nt(keys, q_all[2048:, :]), HIDDEN)
-        scores[rows, 2048:] = s
-        peaks[:, 2048:] = jnp.maximum(peaks[:, 2048:], top(s))
+        weigh_part(p, pl.ds(2048, WIDE), jnp.where(key_at <= prompt_at, nt(keys, q_all[2048:, :]), HIDDEN))
         kpt[:, rows] = keys.astype(f32).T.astype(bf16)
 
     score_part(0)
@@ -265,12 +279,26 @@
 
     def score_slot(t, carry):
         at = columns(t, WIDE)
-        s = jnp.where(span_at <= cand_at, nt(ks[t // 2], q_all[at, :]), HIDDEN)
-        scores[PROMPT:, at] = s
-        peaks[:, at] = jnp.maximum(peaks[:, at], top(s))
+        weigh_part(4, at, jnp.where(span_at <= cand_at, nt(ks[t // 2], q_all[at, :]), HIDDEN))
         return carry
 
     lax.fori_loop(0, 4, score_slot, 0, unroll=2)
+
+    def weigh(t, parts):
+        at = columns(t, WIDE)
+        tops = [peaks[p, 0:1, at] for p in range(parts)]
+        peak = functools.reduce(jnp.maximum, tops)
+        lifts = [jnp.exp2((top - peak) * SCALE2) for top in tops]
+        sums = [jnp.sum(shares[p, :, at], axis=0, keepdims=True) for p in range(parts)]
+        share = 1.0 / sum(lift * total for lift, total in zip(lifts, sums))
+        for p in range(parts):
+            lift = lifts[p] * share
+            shares[p, :, at] = jnp.broadcast_to(lift, (8, WIDE))
+            part_halves(p)[:, at] = (part_scores(p)[:, at] * lift).astype(bf16)
+
+    for t in range(4):
+        weigh(t, KEYS // PART)
+    weigh(4, PROMPT // PART)
 
     small[0].wait()
     small[1].wait()
@@ -290,66 +318,6 @@
             for h in range(8):
                 at = i * 1024 + h * 128 + k * 32
                 g_all[at : at + 32, :] = rows[:, h * 128 : (h + 1) * 128]
-    for p in (1, 2, 3):
-        take(mrecv.at[1, p], vq.at[p])
-    for p in range(4):
-        vpt[:, p * PART : (p + 1) * PART] = vq[p].reshape(PART, 128).astype(f32).T.astype(bf16)
-    take(crecv.at[3], vc.at[0])
-    slot_rows(vc, vs, vst)
-
-    def weigh(t, cand, i):
-        at = columns(t, 256)
-        parts = KEYS // PART if cand else PROMPT // PART
-        peak = jnp.max(peaks[:, at], axis=0, keepdims=True)
-        total = jnp.zeros((8, 256), f32)
-        for p in range(parts):
-            rows = slice(p * PART, (p + 1) * PART)
-            e = jnp.exp2((scores[rows, at] - peak) * SCALE2)
-            scores[rows, at] = e
-            total = total + jnp.sum(e.reshape(-1, 8, 256), axis=0)
-        share = 1.0 / jnp.sum(total, axis=0, keepdims=True)
-        shares[:, at] = jnp.broadcast_to(share, (8, 256))
-        for p in range(parts):
-            rows = slice(p * PART, (p + 1) * PART)
-            halves[rows, at] = (scores[rows, at] * share).astype(bf16)
-        out = nn(vpt[...], halves[0:PROMPT, at])
-        if cand:
-            out = out + nn(vst[i], halves[PROMPT:, at])
-            out = jnp.where(cand_at[:, 0:256] < lengths[i], out, 0.0)
-        delta = jnp.sum(out * g_all[at, :].astype(f32).T, axis=0, keepdims=True)
-        deltas[:, at] = jnp.broadcast_to(delta, (8, 256))
-        return out.T
-
-    def put_cand(target, i, pair, rows):
-        for a in range(2):
-            for k in range(4):
-                at = a * 128 + k * 32
-                target[slots[i] * 4 + k, :, columns(pair * 2 + a, 128)] = rows[at : at + 32, :].astype(bf16)
-
-    def give_back(kind, source, target, width, which):
-        here = target.at[:, columns(g, width)]
-        if 0 in which:
-            start([pltpu.make_async_copy(source.at[j], here, brecv.at[kind])])
-            late.append((bsend.at[kind], source.at[pl.ds(0, 7)]))
-            late.append((brecv.at[kind], target))
-        start([remote(source.at[flip(j, d)], here, bsend.at[kind], brecv.at[kind], block[d]) for d in which if d])
-
-    OTHER, OWN = (4, 5, 6, 7), (1, 2, 3, 0)
-    for i, which in enumerate((OTHER, OWN)):
-
-        def weigh_cand(pair, carry, i=i):
-            put_cand(oc, i, pair, weigh(i * 4 + pair, True, i))
-            return carry
-
-        lax.fori_loop(0, 4, weigh_cand, 0, unroll=2)
-        give_back(0, oc, oc_out, 1024, which)
-
-    def weigh_prompt(t, carry):
-        prompt_out[columns(t, 256), :] = weigh(8 + t, False, None)
-        return carry
-
-    lax.fori_loop(0, 2, weigh_prompt, 0, unroll=2)
-
     def cand_terms(sums, target, i):
         for half in range(2):
             for hi in range(4):
@@ -360,7 +328,7 @@
     def slot_terms(others, scale, box, inbox, kind):
         for i in range(2):
             rows = slice(i * 1024, (i + 1) * 1024)
-            cand_terms(nn(halves[PROMPT:, rows], others[rows, :]) * scale, box, i)
+            cand_terms(nn(slot_halves[:, rows], others[rows, :]) * scale, box, i)
         start(
             [
                 remote(box.at[(zhi + n) % 4], inbox.at[n - 1], csend.at[4 + kind], crecv.at[4 + kind], column[2 * n])
@@ -408,30 +376,67 @@
     for p in FARTHEST:
         terms(g_all, 1.0, dvb, dvown, rv, 0, p)
 
-    def grade(values, turned, rows, at):
+    for p in (1, 2, 3):
+        take(mrecv.at[1, p], vq.at[p])
+    for p in range(4):
+        vpt[:, p * PART : (p + 1) * PART] = vq[p].reshape(PART, 128).astype(f32).T.astype(bf16)
+    take(crecv.at[3], vc.at[0])
+    slot_rows(vc, vs, vst)
+
+    oc, dqc, pp = qc_in, gc_in, pp_in
+
+    def attend(t, cand, i):
+        at = columns(t, 256)
+        out = nn(vpt[...], halves[:, at])
+        if cand:
+            out = out + nn(vst[i], slot_halves[:, at])
+            out = jnp.where(cand_at[:, 0:256] < lengths[i], out, 0.0)
+        delta = jnp.sum(out * g_all[at, :].astype(f32).T, axis=0, keepdims=True)
+        deltas[:, at] = jnp.broadcast_to(delta, (8, 256))
+        return out.T
+
+    def put_cand(target, i, pair, rows):
+        for a in range(2):
+            for k in range(4):
+                at = a * 128 + k * 32
+                target[slots[i] * 4 + k, :, columns(pair * 2 + a, 128)] = rows[at : at + 32, :].astype(bf16)
+
+    def give_back(kind, source, target, width, which):
+        here = target.at[:, columns(g, width)]
+        if 0 in which:
+            start([pltpu.make_async_copy(source.at[j], here, brecv.at[kind])])
+            late.append((bsend.at[kind], source.at[pl.ds(0, 7)]))
+            late.append((brecv.at[kind], target))
+        start([remote(source.at[flip(j, d)], here, bsend.at[kind], brecv.at[kind], block[d]) for d in which if d])
+
+    OTHER, OWN = (4, 5, 6, 7), (1, 2, 3, 0)
+    for i, which in enumerate((OTHER, OWN)):
+
+        for pair in range(4):
+            put_cand(oc, i, pair, attend(i * 4 + pair, True, i))
+        give_back(0, oc, oc_out, 1024, which)
+
+    for t in range(2):
+        prompt_out[columns(t, 256), :] = attend(8 + t, False, None)
+
+    def grade(values, turned, p, at):
         dw = nt(values, g_all[at, :])
-        ds = (scores[rows, at] * shares[0:1, at] * (dw - deltas[0:1, at])).astype(bf16)
-        halves[rows, at] = ds
+        ds = (part_scores(p)[:, at] * shares[p, 0:1, at] * (dw - deltas[0:1, at])).astype(bf16)
+        part_halves(p)[:, at] = ds
         return nn(turned, ds)
 
-    def grade_slot(t, carry):
+    for t in range(4):
         at = columns(t, WIDE)
-        dq[:, at] = grade(vs[t // 2], kst[t // 2], slice(PROMPT, KEYS), at)
-        return carry
-
-    lax.fori_loop(0, 4, grade_slot, 0, unroll=2)
+        dq[:, at] = grade(vs[t // 2], kst[t // 2], 4, at)
     dq[:, 2048:] = jnp.zeros((128, WIDE), f32)
     slot_terms(q_all, SCALE, dkc, ck_in, 1)
 
     def grade_part(p, first, last):
         rows = slice(p * PART, (p + 1) * PART)
 
-        def body(t, carry):
+        for t in range(first, last):
             at = columns(t, WIDE)
-            dq[:, at] += grade(vq[p].reshape(PART, 128), kpt[:, rows], rows, at)
-            return carry
-
-        lax.fori_loop(first, last, body, 0, unroll=2)
+            dq[:, at] += grade(vq[p].reshape(PART, 128), kpt[:, rows], p, at)
 
     for n, p in enumerate(FARTHEST[:3]):
         grade_part(p, 0, 5)
@@ -468,17 +473,28 @@
         take(sem, ref)
 
 
-def finish_kernel(oc, dqc, pp, kvp, ck, cv, prompt_out, prompt_dq, prompt_dk, prompt_dv, oc_out, dqc_out, ck_out, cv_out, sems):
-    copies = [
-        pltpu.make_async_copy(source, target, sems.at[i])
-        for i, (source, target) in enumerate(((oc, oc_out), (dqc, dqc_out), (ck, ck_out), (cv, cv_out)))
+def finish_kernel(
+    oc, dqc, pp, kvp, ck, cv, prompt_out, prompt_dq, prompt_dk, prompt_dv, oc_out, dqc_out, ck_out, cv_out,
+    oc_in, dqc_in, pp_in, kvp_in, ck_in, cv_in, sems,
+):
+    arrive = [
+        pltpu.make_async_copy(source, here, sems.at[i])
+        for i, (source, here) in enumerate(
+            ((oc, oc_in), (dqc, dqc_in), (pp, pp_in), (kvp, kvp_in), (ck, ck_in), (cv, cv_in))
+        )
     ]
-    start(copies)
-    for source, upper, lower in ((pp, prompt_out, prompt_dq), (kvp, prompt_dk, prompt_dv)):
+    start(arrive)
+    leave = []
+    for i, here, target in ((0, oc_in, oc_out), (1, dqc_in, dqc_out), (4, ck_in, ck_out), (5, cv_in, cv_out)):
+        arrive[i].wait()
+        leave.append(pltpu.make_async_copy(here, target, sems.at[6 + i]))
+        leave[-1].start()
+    for i, source, upper, lower in ((2, pp_in, prompt_out, prompt_dq), (3, kvp_in, prompt_dk, prompt_dv)):
+        arrive[i].wait()
         both = source[...].astype(f32)
         upper[...] = both[0:8].astype(bf16)
         lower[...] = both[8:16].astype(bf16)
-    for copy in copies:
+    for copy in leave:
         copy.wait()
 
 
@@ -512,19 +528,18 @@
             half(8, 32, 1024), half(8, 16, 1024), half(8, 32, 1024), half(4, 8, 64, 128), half(4, 8, 64, 128),
             half(LANES, 128), half(LANES, 128), half(2, SPAN, 128), half(2, SPAN, 128),
             half(128, PROMPT), half(128, PROMPT), half(2, 128, SPAN), half(2, 128, SPAN),
-            full(KEYS, LANES), half(KEYS, LANES), full(8, LANES), full(8, LANES), full(8, LANES), full(512, 128), full(128, LANES),
-            half(8, 32, 1024), half(8, 32, 1024), half(8, 16, 1024),
+            full(PROMPT, LANES), half(PROMPT, LANES), full(SPAN, 2048), half(SPAN, 2048), full(5, 8, LANES), full(5, 8, LANES), full(8, LANES), full(512, 128), full(128, LANES),
             half(3, 8, 64, 128), half(3, 8, 64, 128), half(3, 8, 64, 128), half(3, 8, 64, 128),
             half(8, 64, 128), half(8, 64, 128), half(7, 64, 128), half(7, 64, 128),
             full(8, 64, 128), full(8, 64, 128), full(64, 128),
             half(4, 8, 32, 128), half(4, 8, 32, 128), half(3, 8, 32, 128), half(3, 8, 32, 128),
             half(8, 32, 128), half(8, 32, 128), half(8, 16, 128),
             pltpu.SMEM((16,), jnp.int32), pltpu.SMEM((16,), jnp.int32),
-            DMA((2,)), DMA((6,)), DMA((6,)), DMA((4,)), DMA((4,)), DMA((4,)), DMA((4, 4)),
+            DMA((2,)), DMA((6,)), DMA((6,)), DMA((4,)), DMA((6,)), DMA((4,)), DMA((4, 4)),
             DMA((6,)), DMA((6,)), DMA((6,)), DMA((6,)),
         ],
         compiler_params=pltpu.CompilerParams(
-            collective_id=0, has_side_effects=True, vmem_limit_bytes=56 * 2**20
+            collective_id=0, has_side_effects=True, vmem_limit_bytes=60 * 2**20
         ),
         name="layer",
     )(
@@ -537,9 +552,11 @@
             result(8, 8192), result(8, 8192), result(8, 1024), result(8, 1024),
             result(32, 8192), result(32, 8192), result(32, 1024), result(32, 1024),
         ),
-        in_specs=[VMEM] * 6,
+        in_specs=[ANY] * 6,
         out_specs=(VMEM,) * 4 + (ANY,) * 4,
-        scratch_shapes=[DMA((4,))],
+        scratch_shapes=[
+            half(32, 8192), half(32, 8192), half(16, 8192), half(16, 1024), half(32, 1024), half(32, 1024), DMA((12,))
+        ],
         name="finish",
     )(oc, dqc, pp, kvp, ck, cv)
 

time: 80.7 us -> 77.2 us (0.957)
  Pallas kernels: 79.8 us -> 76.2 us
    pallas_call x1, Pallas kernels: 76.7 us -> 73.4 us  [local(): pl.pallas_call(kernel, out_shape=(result(32, 8192), result(32, 8192), res...]
where the time goes in v5:
time: 77.2 us; the launch traced here: 77 us
  Pallas kernels  76.2 us (99%)
  between operations  0.83 us (1%)
    pallas_call x1, Pallas kernels, local(): pl.pallas_call(kernel, out_shape=(result(32, 8192), result(32, 8192), res...  73.4 us
    pallas_call x1, Pallas kernels, local(): pl.pallas_call(finish_kernel, out_shape=(result(8, 8192), result(8, 8192)...  2.85 us

profile of v5, /device:TPU:1, one launch (start us, length us, event | category | flops | bytes accessed | tf_op | source)
XLA Modules:
  0.0 77.0 jit_solution(17757025596198244113)
XLA Ops:
  0.6 73.4 %layer.1 = (bf16[32,8192]{1,0:T(8,128)(2,1)}, bf16[32,8192]{1,0:T(8,128)(2,1)}, bf16[16,8192]{1,0:T(8,128)(2,1)}, bf16[16,1024]{1,0:T(8,128)(2,1)}, bf16[32,1024]{1,0:T(8,128)(2,1)}, /*index=5*/bf16[32,1024]{1,0:T(8,128)(2,1)}) custom-call(s32[16]{0:T(128)} %cand_len_in.1, s32[16]{0:T(128)} %placement_in.1, bf16[8,8192]{1,0:T(8,128)(2,1)} %prompt_q.1, ...), custom_call_target="tpu_custom_call" | custom-call | tf_op jit(solution)/shard_map/layer/pallas_call | solution.py:519
  74.0 2.8 %finish.1 = (bf16[8,8192]{1,0:T(8,128)(2,1)}, bf16[8,8192]{1,0:T(8,128)(2,1)}, bf16[8,1024]{1,0:T(8,128)(2,1)}, bf16[8,1024]{1,0:T(8,128)(2,1)}, bf16[32,8192]{1...) custom-call(bf16[32,8192]{1,0:T(8,128)(2,1)} %get-tuple-element.14.oc, ...), custom_call_target="tpu_custom_call" | custom-call | tf_op jit(solution)/shard_map/finish/pallas_call | solution.py:549

commit v6 on v5

--- a/solution.py
+++ b/solution.py
@@ -194,12 +194,12 @@
     kq[0, z] = both[:, 0:8, :].reshape(64, 128).astype(bf16)
     vq[0, z] = both[:, 8:16, :].reshape(64, 128).astype(bf16)
     along_z_in(kq, 0)
+    along_z_in(vq, 1)
     near(kc, 0)
-    along_z_in(vq, 1)
     quadrants(kq, 0)
+    quadrants(vq, 1)
     far(kc, 0)
     near(vc, 1)
-    quadrants(vq, 1)
 
     slots = (1 - sy, sy)
     take(arecv.at[2], qc_in)

time: 77.2 us -> 76.3 us (0.988)
  Pallas kernels: 76.2 us -> 75.4 us
    pallas_call x1, Pallas kernels: 73.4 us -> 72.5 us  [local(): pl.pallas_call(kernel, out_shape=(result(32, 8192), result(32, 8192), res...]
where the time goes in v6:
time: 76.3 us; the launch traced here: 76.2 us
  Pallas kernels  75.4 us (99%)
  between operations  0.83 us (1%)
    pallas_call x1, Pallas kernels, local(): pl.pallas_call(kernel, out_shape=(result(32, 8192), result(32, 8192), res...  72.5 us
    pallas_call x1, Pallas kernels, local(): pl.pallas_call(finish_kernel, out_shape=(result(8, 8192), result(8, 8192)...  2.85 us

profile of v6, /device:TPU:1, one launch (start us, length us, event | category | flops | bytes accessed | tf_op | source)
XLA Modules:
  0.0 76.2 jit_solution(1557894723513448659)
XLA Ops:
  0.6 72.5 %layer.1 = (bf16[32,8192]{1,0:T(8,128)(2,1)}, bf16[32,8192]{1,0:T(8,128)(2,1)}, bf16[16,8192]{1,0:T(8,128)(2,1)}, bf16[16,1024]{1,0:T(8,128)(2,1)}, bf16[32,1024]{1,0:T(8,128)(2,1)}, /*index=5*/bf16[32,1024]{1,0:T(8,128)(2,1)}) custom-call(s32[16]{0:T(128)} %cand_len_in.1, s32[16]{0:T(128)} %placement_in.1, bf16[8,8192]{1,0:T(8,128)(2,1)} %prompt_q.1, ...), custom_call_target="tpu_custom_call" | custom-call | tf_op jit(solution)/shard_map/layer/pallas_call | solution.py:519
  73.2 2.8 %finish.1 = (bf16[8,8192]{1,0:T(8,128)(2,1)}, bf16[8,8192]{1,0:T(8,128)(2,1)}, bf16[8,1024]{1,0:T(8,128)(2,1)}, bf16[8,1024]{1,0:T(8,128)(2,1)}, bf16[32,8192]{1...) custom-call(bf16[32,8192]{1,0:T(8,128)(2,1)} %get-tuple-element.14.oc, ...), custom_call_target="tpu_custom_call" | custom-call | tf_op jit(solution)/shard_map/finish/pallas_call | solution.py:549
